TPU v7x, 256 devices: a whole 4x4x8 slice. The times are simulated.
256 devices in a mesh: seq: 32 (over z, x_lo, core), chan: 8 (over x_hi, y).
Axes of the slice: x: 4 (x_hi: 2, x_lo: 2; x = x_hi * 2 + x_lo), y: 4, z: 8, core: 2. Of those that a mesh axis runs over, the one named last changes fastest.
Arguments:
- query_rows: bfloat16 [16384, 4096], P('seq', 'chan'), may hold values from -6 to 6
- key_rows: bfloat16 [16384, 4096], P('seq', 'chan'), may hold values from -6 to 6
- value_rows: bfloat16 [16384, 4096], P('seq', 'chan'), may hold values from -6 to 6
- filter_taps: float32 [16384, 4096], P('seq', 'chan'), may hold values from -1 to 1
- skip_gain: float32 [4096], P('chan'), may hold values from 0.5 to 1.5
- w_out: bfloat16 [4096, 8192], P('chan'), may hold values from -0.09375 to 0.09375
Outputs:
- mixed: bfloat16 [16384, 8192], P('seq', 'chan')
All inputs are finite; a program needn't handle non-finite values.
Results may differ from a plain program's by a relative error of at most 0.005.
Values may be sent and summed in bfloat16 or wider, within the bound.
A program may use at most 192 MiB of HBM per device.

v0:
```python
import math

import jax
import jax.numpy as jnp
from jax import lax
from jax.sharding import PartitionSpec as P


def rotation(first_idx, second_idx, period, sign):
    residue = first_idx * second_idx % period
    phase_angle = residue.astype(jnp.float32) * (sign * 2.0 * math.pi / period)
    return (jnp.cos(phase_angle), jnp.sin(phase_angle))


def table(count_out, count_in, period, sign):
    first_idx = lax.broadcasted_iota(jnp.int32, (count_out, count_in), 0)
    second_idx = lax.broadcasted_iota(jnp.int32, (count_out, count_in), 1)
    return rotation(first_idx, second_idx, period, sign)


def complex_einsum(formula, cosine, sine, real_part, imag_part):
    exact = lax.Precision.HIGHEST
    real_out = jnp.einsum(formula, cosine, real_part, precision=exact) - jnp.einsum(
        formula, sine, imag_part, precision=exact
    )
    imag_out = jnp.einsum(formula, sine, real_part, precision=exact) + jnp.einsum(
        formula, cosine, imag_part, precision=exact
    )
    return (real_out, imag_out)


def twist(cosine, sine, real_part, imag_part):
    return (cosine * real_part - sine * imag_part, sine * real_part + cosine * imag_part)


def distributed_convolution(product, filter_taps, seq_count):
    exact = lax.Precision.HIGHEST
    rows_local = product.shape[0]
    channels = product.shape[1]
    block_rows = rows_local // seq_count
    padded_len = 2 * seq_count * rows_local
    own_index = lax.axis_index("seq")
    stacked = jnp.stack((product, filter_taps)).reshape(2, seq_count, block_rows, channels)
    columns = lax.all_to_all(stacked, "seq", split_axis=1, concat_axis=1, tiled=True)
    lane_half = lax.broadcasted_iota(jnp.int32, (2, seq_count, seq_count), 0)
    lane_freq = lax.broadcasted_iota(jnp.int32, (2, seq_count, seq_count), 1)
    lane_source = lax.broadcasted_iota(jnp.int32, (2, seq_count, seq_count), 2)
    cosine, sine = rotation(lane_freq + seq_count * lane_half, lane_source, 2 * seq_count, -1.0)
    spec_real = jnp.einsum("erm,wmbc->werbc", cosine, columns, precision=exact)
    spec_imag = jnp.einsum("erm,wmbc->werbc", sine, columns, precision=exact)
    spec_real, spec_imag = (
        lax.all_to_all(spec_real, "seq", split_axis=2, concat_axis=2, tiled=True),
        lax.all_to_all(spec_imag, "seq", split_axis=2, concat_axis=2, tiled=True),
    )
    spec_real = spec_real.reshape(2, 2, rows_local, channels)
    spec_imag = spec_imag.reshape(2, 2, rows_local, channels)
    half_idx = lax.broadcasted_iota(jnp.int32, (2, rows_local, 1), 0)
    pos_idx = lax.broadcasted_iota(jnp.int32, (2, rows_local, 1), 1)
    freq_own = own_index + seq_count * half_idx
    cosine, sine = rotation(freq_own, pos_idx, padded_len, -1.0)
    spec_real, spec_imag = twist(cosine, sine, spec_real, spec_imag)
    spec_real = spec_real.reshape(2, 2, seq_count, block_rows, channels)
    spec_imag = spec_imag.reshape(2, 2, seq_count, block_rows, channels)
    cosine, sine = table(seq_count, seq_count, seq_count, -1.0)
    spec_real, spec_imag = complex_einsum("kj,wejbc->wekbc", cosine, sine, spec_real, spec_imag)
    cosine, sine = table(seq_count, block_rows, rows_local, -1.0)
    spec_real, spec_imag = twist(cosine[:, :, None], sine[:, :, None], spec_real, spec_imag)
    cosine, sine = table(block_rows, block_rows, block_rows, -1.0)
    spec_real, spec_imag = complex_einsum("lb,wekbc->weklc", cosine, sine, spec_real, spec_imag)
    prod_real = spec_real[0] * spec_real[1] - spec_imag[0] * spec_imag[1]
    prod_imag = spec_real[0] * spec_imag[1] + spec_imag[0] * spec_real[1]
    cosine, sine = table(block_rows, block_rows, block_rows, 1.0)
    prod_real, prod_imag = complex_einsum("bl,eklc->ekbc", cosine, sine, prod_real, prod_imag)
    cosine, sine = table(seq_count, block_rows, rows_local, 1.0)
    prod_real, prod_imag = twist(cosine[:, :, None], sine[:, :, None], prod_real, prod_imag)
    cosine, sine = table(seq_count, seq_count, seq_count, 1.0)
    prod_real, prod_imag = complex_einsum("jk,ekbc->ejbc", cosine, sine, prod_real, prod_imag)
    prod_real = prod_real.reshape(2, rows_local, channels)
    prod_imag = prod_imag.reshape(2, rows_local, channels)
    cosine, sine = rotation(freq_own, pos_idx, padded_len, 1.0)
    prod_real, prod_imag = twist(cosine, sine, prod_real, prod_imag)
    prod_real = prod_real.reshape(2, seq_count, block_rows, channels)
    prod_imag = prod_imag.reshape(2, seq_count, block_rows, channels)
    prod_real, prod_imag = (
        lax.all_to_all(prod_real, "seq", split_axis=1, concat_axis=1, tiled=True),
        lax.all_to_all(prod_imag, "seq", split_axis=1, concat_axis=1, tiled=True),
    )
    target_idx = lax.broadcasted_iota(jnp.int32, (seq_count, 2, seq_count), 0)
    back_half = lax.broadcasted_iota(jnp.int32, (seq_count, 2, seq_count), 1)
    back_freq = lax.broadcasted_iota(jnp.int32, (seq_count, 2, seq_count), 2)
    cosine, sine = rotation(target_idx, back_freq + seq_count * back_half, 2 * seq_count, 1.0)
    conv_rows = jnp.einsum("mer,erbc->mbc", cosine, prod_real, precision=exact)
    conv_rows = conv_rows - jnp.einsum("mer,erbc->mbc", sine, prod_imag, precision=exact)
    conv_rows = conv_rows * (1.0 / padded_len)
    return lax.all_to_all(conv_rows, "seq", split_axis=0, concat_axis=0, tiled=True).reshape(
        rows_local, channels
    )


def on_device(query_rows, key_rows, value_rows, filter_taps, skip_gain, w_out):
    seq_count = lax.axis_size("seq")
    product = key_rows.astype(jnp.float32) * value_rows.astype(jnp.float32)
    conv_rows = distributed_convolution(product, filter_taps, seq_count)
    gated = (query_rows.astype(jnp.float32) * (conv_rows + skip_gain * product)).astype(
        jnp.bfloat16
    )
    partial_value = jnp.dot(gated, w_out, preferred_element_type=jnp.float32)
    mixed = lax.psum_scatter(partial_value, "chan", scatter_dimension=1, tiled=True)
    return mixed.astype(jnp.bfloat16)


def solution(mesh):
    return jax.shard_map(
        on_device,
        mesh=mesh,
        in_specs=(
            P("seq", "chan"),
            P("seq", "chan"),
            P("seq", "chan"),
            P("seq", "chan"),
            P("chan"),
            P("chan", None),
        ),
        out_specs=P("seq", "chan"),
        check_vma=False,
    )
```

profile of v0, /device:TPU:2, one launch (start us, length us, event | category | flops | bytes accessed | tf_op | source)
XLA Modules:
  0.0 741.3 jit_solution(13985472079795141320)
XLA Ops:
  6.5 1.4 convert_multiply_fusion
  8.0 0.1 copy-done.2
  8.1 0.3 pad_maximum_fusion
  8.4 1.6 copy.48
  10.0 10.1 %all-to-all-start = ((f32[2,32,16,512]{3,2,0,1:T(8,128)}), f32[2,32,16,512]{3,2,0,1:T(8,128)S(1)}, u32[]{:S(2)}, u32[]{:S(2)}) async-start(f32[2,32,16,512]{3,2,0,1:T(8,128)} %copy.48), calls=%async_computation | async-start | bytes 4194304 | tf_op jit(solution)/shard_map/all_to_all | solution.py:44
  20.1 50.2 %all-to-all-done = f32[2,32,16,512]{3,2,0,1:T(8,128)S(1)} async-done(((f32[2,32,16,512]{3,2,0,1:T(8,128)}), f32[2,32,16,512]{3,2,0,1:T(8,128)S(1)}, u32[]{:S(2)}, u32[]{:S(2)}) %all-to-all-start) | async-done | bytes 2097184 | tf_op jit(solution)/shard_map/all_to_all | solution.py:44
  70.3 5.4 convolution_bitcast_fusion
  75.7 5.2 copy.53
  81.0 5.4 all-to-all-start.2
  86.4 5.4 convolution_bitcast_fusion.1
  91.8 5.2 copy.50
  97.1 83.3 %all-to-all-done.2 = f32[2,2,32,16,512]{4,1,3,0,2:T(2,128)} async-done(((f32[2,2,32,16,512]{4,1,3,0,2:T(2,128)}), f32[2,2,32,16,512]{4,1,3,0,2:T(2,128)}, u32[]{:S(2)}, u32[]{:S(2)}) %all-to-all-start.2) | async-done | bytes 4194336 | tf_op jit(solution)/shard_map/all_to_all | solution.py:53
  180.3 7.4 %all-to-all-start.1 = ((f32[2,2,32,16,512]{4,1,3,0,2:T(2,128)}), f32[2,2,32,16,512]{4,1,3,0,2:T(2,128)}, u32[]{:S(2)}, u32[]{:S(2)}) async-start(f32[2,2,32,16,512]{4,1,3,0,2:T(2,128)} %copy.50), calls=%async_computation.1 | async-start | bytes 8388608 | tf_op jit(solution)/shard_map/all_to_all | solution.py:52
  187.8 0.1 multiply_cosine_fusion.11
  187.8 0.1 copy.46
  187.9 0.1 multiply_sine_fusion.11
  188.0 0.1 copy.62
  188.1 0.2 multiply_cosine_fusion.3
  188.3 0.2 copy.47
  188.5 0.2 copy.51
  188.7 0.1 multiply_sine_fusion.10
  188.8 93.1 %all-to-all-done.1 = f32[2,2,32,16,512]{4,1,3,0,2:T(2,128)} async-done(((f32[2,2,32,16,512]{4,1,3,0,2:T(2,128)}), f32[2,2,32,16,512]{4,1,3,0,2:T(2,128)}, u32[]{:S(2)}, u32[]{:S(2)}) %all-to-all-start.1) | async-done | bytes 4194336 | tf_op jit(solution)/shard_map/all_to_all | solution.py:52
  281.9 6.4 multiply_subtract_fusion
  288.3 7.1 fusion.10
  295.5 7.3 fusion.12
  302.7 7.5 %fusion.18 = f32[2,2,16,512,32]{3,4,2,1,0:T(8,128)S(1)} fusion(f32[2,2,16,512,32]{3,4,2,1,0:T(8,128)S(1)} %fusion.12, f32[2,2,32,16,512]{4,1,3,0,2:T(2,128)S(1)} %get-tuple-element.5), kind=kOutput, calls=%fused_computation.26 | convolution fusion | flops 403716096 | bytes 12582912 | tf_op jit(solution)/shard_map/kj,wejbc->wekbc/dot_general | solution.py:23
  310.3 9.4 %fusion = (f32[2,2,32,16,512]{4,2,3,1,0:T(8,128)S(1)}, f32[2,2,32,16,512]{4,2,3,1,0:T(8,128)S(1)}) fusion(f32[2,2,16,512,32]{3,4,2,1,0:T(8,128)S(1)} %fusion.18, f32[32,16]{0,1:T(8,128)S(1)} %get-tuple-element.19, f32[32,16]{0,1:T(8,128)S(1)} %get-tuple-element.20, f32[2,2,16,512,32]{3,4,2,1,0:T(8,128)S(1)} %fusion.10, ...), kind=kOutput, calls=%fused_computation.2 | convolution fusion | flops 410007552 | bytes 20975616 | tf_op jit(solution)/shard_map/kj,wejbc->wekbc/dot_general | solution.py:26
  319.7 6.6 fusion.2
  326.3 6.7 fusion.4
  333.0 7.4 subtract_bitcast_fusion
  340.4 7.1 add_bitcast_fusion
  347.5 1.1 multiply_subtract_fusion.1
  348.6 2.1 fusion.30
  350.7 2.5 fusion.32
  353.2 2.3 fusion.58
  355.4 2.9 subtract_bitcast_fusion.1
  358.4 3.3 fusion.44
  361.7 3.5 fusion.46
  365.2 3.5 fusion.52
  368.7 4.1 fusion.29
  372.8 2.5 copy.67
  375.3 7.3 all-to-all-start.3
  382.7 2.6 copy.69
  385.2 49.0 %all-to-all-done.3 = f32[2,32,16,512]{3,2,0,1:T(8,128)} async-done(((f32[2,32,16,512]{3,2,0,1:T(8,128)}), f32[2,32,16,512]{3,2,0,1:T(8,128)}, u32[]{:S(2)}, u32[]{:S(2)}) %all-to-all-start.3) | async-done | bytes 2097184 | tf_op jit(solution)/shard_map/all_to_all | solution.py:85
  434.3 4.2 all-to-all-start.4
  438.4 0.3 reduce-scatter.2.cloned.1.call-start
  438.7 4.0 fusion.64
  442.7 47.3 %all-to-all-done.4 = f32[2,32,16,512]{3,2,0,1:T(8,128)S(1)} async-done(((f32[2,32,16,512]{3,2,0,1:T(8,128)}), f32[2,32,16,512]{3,2,0,1:T(8,128)S(1)}, u32[]{:S(2)}, u32[]{:S(2)}) %all-to-all-start.4) | async-done | bytes 2097184 | tf_op jit(solution)/shard_map/all_to_all | solution.py:86
  490.0 2.5 fusion.73
  492.5 0.0 copy-start
  492.5 0.0 copy-start.1
  492.5 0.0 copy-start.3
  492.5 0.0 copy-start.4
  492.5 0.6 copy.71
  493.2 32.2 %all_to_all.30 = f32[32,16,512]{2,1,0:T(8,128)S(1)} all-to-all(f32[32,16,512]{2,1,0:T(8,128)S(1)} %copy.71), channel_id=1, replica_groups=mesh['seq'=32,'chan'=8] {'seq'}, dimensions={0} | all-to-all | bytes 2097152 | tf_op jit(solution)/shard_map/all_to_all | solution.py:95
  525.4 0.0 copy-done
  525.4 0.0 copy-done.1
  525.4 0.0 copy-done.3
  525.4 0.0 copy-done.4
  525.4 0.3 fusion.77
  525.7 11.6 %fusion.265 = f32[512,8192]{1,0:T(8,128)} fusion(bf16[512,512]{1,0:T(8,128)(2,1)S(1)} %fusion.77, bf16[512,8192]{1,0:T(8,128)(2,1)} %param.11), kind=kOutput, calls=%fused_computation.277 | convolution fusion | flops 4294967296 | bytes 25690112 | tf_op jit(solution)/shard_map/dot_general | solution.py:107
  537.3 0.0 reduce-scatter.2.cloned.1.call-update
  537.3 194.2 %reduce-scatter.2.cloned.1.call-done = f32[512,1024]{1,0:T(8,128)} async-done(((f32[512,8192]{1,0:T(8,128)}), f32[512,1024]{1,0:T(8,128)}) %reduce-scatter.2.cloned.1.call-update) | async-done | bytes 2097168 | tf_op jit(solution)/shard_map/reduce_scatter | solution.py:108
  731.5 2.7 convert_element_type.124
  (4 shorter events, 0.0 us)
Async XLA Ops:
  6.5 1.5 copy-start.2
  10.0 60.3 %all-to-all-start = ((f32[2,32,16,512]{3,2,0,1:T(8,128)}), f32[2,32,16,512]{3,2,0,1:T(8,128)S(1)}, u32[]{:S(2)}, u32[]{:S(2)}) async-start(f32[2,32,16,512]{3,2,0,1:T(8,128)} %copy.48), calls=%async_computation | async-start | bytes 4194304 | tf_op jit(solution)/shard_map/all_to_all | solution.py:44
  81.0 99.3 %all-to-all-start.2 = ((f32[2,2,32,16,512]{4,1,3,0,2:T(2,128)}), f32[2,2,32,16,512]{4,1,3,0,2:T(2,128)}, u32[]{:S(2)}, u32[]{:S(2)}) async-start(f32[2,2,32,16,512]{4,1,3,0,2:T(2,128)} %copy.53), calls=%async_computation.2 | async-start | bytes 8388608 | tf_op jit(solution)/shard_map/all_to_all | solution.py:53
  180.3 101.5 %all-to-all-start.1 = ((f32[2,2,32,16,512]{4,1,3,0,2:T(2,128)}), f32[2,2,32,16,512]{4,1,3,0,2:T(2,128)}, u32[]{:S(2)}, u32[]{:S(2)}) async-start(f32[2,2,32,16,512]{4,1,3,0,2:T(2,128)} %copy.50), calls=%async_computation.1 | async-start | bytes 8388608 | tf_op jit(solution)/shard_map/all_to_all | solution.py:52
  375.3 58.9 %all-to-all-start.3 = ((f32[2,32,16,512]{3,2,0,1:T(8,128)}), f32[2,32,16,512]{3,2,0,1:T(8,128)}, u32[]{:S(2)}, u32[]{:S(2)}) async-start(f32[2,32,16,512]{3,2,0,1:T(8,128)} %copy.67), calls=%async_computation.3 | async-start | bytes 4194304 | tf_op jit(solution)/shard_map/all_to_all | solution.py:85
  434.3 55.7 %all-to-all-start.4 = ((f32[2,32,16,512]{3,2,0,1:T(8,128)}), f32[2,32,16,512]{3,2,0,1:T(8,128)S(1)}, u32[]{:S(2)}, u32[]{:S(2)}) async-start(f32[2,32,16,512]{3,2,0,1:T(8,128)} %copy.69), calls=%async_computation.4 | async-start | bytes 4194304 | tf_op jit(solution)/shard_map/all_to_all | solution.py:86
  438.4 293.1 %reduce-scatter.2.cloned.1.call-start = ((), (), s32[]{:S(2)}) async-start(), calls=%async_computation.7 | async-start | bytes 18874368 | tf_op jit(solution)/shard_map/reduce_scatter | solution.py:108
  492.5 32.9 %copy-start = (bf16[512,512]{1,0:T(8,128)(2,1)S(1)}, bf16[512,512]{1,0:T(8,128)(2,1)}, u32[]{:S(2)}) copy-start(bf16[512,512]{1,0:T(8,128)(2,1)} %param.8) | copy-start | bytes 1572868
  492.5 32.9 %copy-start.1 = (bf16[512,512]{1,0:T(8,128)(2,1)S(1)}, bf16[512,512]{1,0:T(8,128)(2,1)}, u32[]{:S(2)}) copy-start(bf16[512,512]{1,0:T(8,128)(2,1)} %param.7) | copy-start | bytes 1572868
  492.5 32.8 %copy-start.3 = (bf16[512,512]{1,0:T(8,128)(2,1)S(1)}, bf16[512,512]{1,0:T(8,128)(2,1)}, u32[]{:S(2)}) copy-start(bf16[512,512]{1,0:T(8,128)(2,1)} %param.6) | copy-start | bytes 1572868
  492.5 32.8 %copy-start.4 = (f32[512]{0:T(512)S(1)}, f32[512]{0:T(512)}, u32[]{:S(2)}) copy-start(f32[512]{0:T(512)} %param.10) | copy-start | bytes 6148
Sparse Core Ops, SparseCore 0:
  537.4 194.0 reduce-scatter.1
where the time goes:
time: 749 us; the launch traced here: 741 us
  waiting for transfers between devices  517 us (69%)
  matrix products  112 us (15%)
  starting transfers between devices  34.7 us (5%)
  blocking collectives  32.2 us (4%)
  local copies, waits for them, and re-layouts  18.4 us (2%)
  between operations  14 us (2%)
  other arithmetic  12.7 us (2%)
    reduce_scatter x1, waiting for transfers between devices, on_device(): lax.psum_scatter(partial_value, 'chan', scatter_dimension=1, tiled=True)  194 us
    all_to_all x1, waiting for transfers between devices, distributed_convolution(): lax.all_to_all(spec_real, 'seq', split_axis=2, concat_axis=2, tiled=True)  93.1 us
    all_to_all x1, waiting for transfers between devices, distributed_convolution(): lax.all_to_all(spec_imag, 'seq', split_axis=2, concat_axis=2, tiled=True)  83.3 us
    all_to_all x1, waiting for transfers between devices, distributed_convolution(): lax.all_to_all(stacked, 'seq', split_axis=1, concat_axis=1, tiled=True)  50.2 us
    all_to_all x1, waiting for transfers between devices, distributed_convolution(): lax.all_to_all(prod_real, 'seq', split_axis=1, concat_axis=1, tiled=True)  49 us
    all_to_all x1, waiting for transfers between devices, distributed_convolution(): lax.all_to_all(prod_imag, 'seq', split_axis=1, concat_axis=1, tiled=True)  47.3 us
    all_to_all x1, blocking collectives, distributed_convolution(): lax.all_to_all(conv_rows, 'seq', split_axis=0, concat_axis=0, tiled=True)  32.2 us
    dot_general x4, matrix products, complex_einsum(): jnp.einsum(formula, sine, real_part, precision=exact)  23.5 us
  transfers between devices with their start and end apart: 6, of which 6 were waited for; matrix products, arithmetic and copies ran while one was open for 2% of the time, Pallas kernels for 0%

commit v1 on v0

v1 whole, which is shorter than its diff:
```python
import functools

import jax
import jax.numpy as jnp
import ml_dtypes
import numpy as np
from jax import lax
from jax.experimental import pallas as pl
from jax.experimental.pallas import tpu as pltpu
from jax.sharding import PartitionSpec as P

MESH = pl.DeviceIdType.MESH
LANES = 128
CHUNKS = 2
BF16 = jnp.bfloat16
F32 = jnp.float32


def split_table(table):
    high = table.astype(ml_dtypes.bfloat16)
    low = (table - high.astype(np.float64)).astype(ml_dtypes.bfloat16)
    return high, low


def transform_tables(seq_count, row_groups):
    coarse = seq_count * row_groups
    total = coarse * LANES
    freq = np.arange(coarse) + 0.25
    order = (np.arange(seq_count)[None, :] * row_groups + np.arange(row_groups)[:, None]).reshape(-1)
    angle = 2.0 * np.pi * freq[:, None] * order[None, :] / coarse
    forward_first = np.concatenate((np.cos(angle), -np.sin(angle)), axis=0)
    inverse_first = np.concatenate((np.cos(angle).T, -np.sin(angle).T), axis=1) / total
    fine = np.arange(LANES)
    turn = 2.0 * np.pi * freq[:, None] * fine[None, :] / total
    twist_cos = np.cos(turn).astype(np.float32)
    twist_sin = np.sin(turn).astype(np.float32)
    inner = 2.0 * np.pi * (fine[:, None] * fine[None, :] % LANES) / LANES
    cosine, sine = np.cos(inner), np.sin(inner)
    forward_second = np.block([[cosine, -sine], [sine, cosine]])
    inverse_second = np.block([[cosine, sine], [-sine, cosine]])
    return (
        np.concatenate(split_table(forward_first), axis=1),
        twist_cos,
        twist_sin,
        *split_table(forward_second),
        *split_table(inverse_second),
        *split_table(inverse_first),
    )


def mm(left, right):
    return jnp.dot(left, right, preferred_element_type=F32)


def mm_nt(left, right):
    return lax.dot_general(left, right, (((1,), (1,)), ((), ())), preferred_element_type=F32)


def split(value):
    high = value.astype(BF16)
    low = (value - high.astype(F32)).astype(BF16)
    return high, low


def eye(size):
    row = lax.broadcasted_iota(jnp.int32, (size, size), 0)
    col = lax.broadcasted_iota(jnp.int32, (size, size), 1)
    return (row == col).astype(F32).astype(BF16)


def kernel(
    seq_count, chan_count,
    q_ref, k_ref, v_ref, h_ref, skip_ref, w_ref,
    first_ref, tcos_ref, tsin_ref, sec_hi, sec_lo, isec_hi, isec_lo, ifirst_hi, ifirst_lo,
    out_ref,
    send, recv, staged, ysend, yrecv, ybuf, gown, gall, wall, acc,
    send_sem, recv_sem, ysend_sem, yrecv_sem, gsend_sem, grecv_sem,
    wsend_sem, wrecv_sem, fsend_sem, frecv_sem, wown_sem,
):
    rows, channels = q_ref.shape
    groups = rows // LANES
    width = channels // CHUNKS
    per = width // seq_count
    coarse = seq_count * groups
    cols = out_ref.shape[1]
    half_rows = channels // 2
    y_count = chan_count // 2
    me = lax.axis_index("seq")
    chan = lax.axis_index("chan")
    core = me % 2
    flipped = me + 2 - 4 * ((me // 2) % 2)
    x_hi = chan // y_count
    sibling = me + 1 - 2 * core

    def w_peer(j):
        other = (chan + j) % chan_count
        seq_to = jnp.where(other // y_count == x_hi, me, flipped)
        return other, seq_to

    barrier = pltpu.get_barrier_semaphore()

    @pl.loop(1, seq_count)
    def _(j):
        pl.semaphore_signal(barrier, inc=1, device_id={"seq": (me + j) % seq_count, "chan": chan}, device_id_type=MESH)

    @pl.loop(1, chan_count)
    def _(j):
        pl.semaphore_signal(barrier, inc=1, device_id={"seq": me, "chan": (chan + j) % chan_count}, device_id_type=MESH)

    @pl.loop(0, y_count)
    def _(j):
        other = ((1 - x_hi) * y_count) + j
        pl.semaphore_signal(barrier, inc=1, device_id={"seq": flipped, "chan": other}, device_id_type=MESH)

    def prepare(n):
        cut = slice(n * width, (n + 1) * width)
        unit = eye(width)
        product = (k_ref[:, cut].astype(F32) * v_ref[:, cut].astype(F32)).astype(BF16)
        p_rows = mm_nt(unit, product).reshape(seq_count, per, rows)
        h_rows = mm_nt(unit, h_ref[:, cut].astype(BF16)).reshape(seq_count, per, rows)
        send[n] = jnp.concatenate((p_rows, h_rows), axis=1).astype(BF16)

    prepare(0)
    pl.semaphore_wait(barrier, seq_count - 1 + chan_count - 1 + y_count)

    def block_copy(n, slot_out, slot_in, to):
        return pltpu.make_async_remote_copy(
            src_ref=send.at[n, slot_out], dst_ref=recv.at[n, slot_in],
            send_sem=send_sem.at[n, slot_out], recv_sem=recv_sem.at[n, slot_in],
            device_id={"seq": to, "chan": chan}, device_id_type=MESH)

    def back_copy(n, slot_out, slot_in, to):
        return pltpu.make_async_remote_copy(
            src_ref=ysend.at[n, slot_out], dst_ref=yrecv.at[n, slot_in],
            send_sem=ysend_sem.at[n, slot_out], recv_sem=yrecv_sem.at[n, slot_in],
            device_id={"seq": to, "chan": chan}, device_id_type=MESH)

    def gated_copy(n, slot_in, other):
        return pltpu.make_async_remote_copy(
            src_ref=gown.at[n], dst_ref=gall.at[n, slot_in],
            send_sem=gsend_sem.at[n, other], recv_sem=grecv_sem.at[n, slot_in],
            device_id={"seq": me, "chan": other}, device_id_type=MESH)

    own_half = pl.ds(pl.multiple_of(core * half_rows, half_rows), half_rows)

    def w_copy(slot_in, other, seq_to):
        return pltpu.make_async_remote_copy(
            src_ref=w_ref.at[own_half, pl.ds(pl.multiple_of(other * cols, cols), cols)],
            dst_ref=wall.at[slot_in, own_half],
            send_sem=wsend_sem.at[other], recv_sem=wrecv_sem.at[slot_in],
            device_id={"seq": seq_to, "chan": other}, device_id_type=MESH)

    def w_share(slot, half):
        part = pl.ds(pl.multiple_of(half * half_rows, half_rows), half_rows)
        return pltpu.make_async_remote_copy(
            src_ref=wall.at[slot, part], dst_ref=wall.at[slot, part],
            send_sem=fsend_sem.at[slot], recv_sem=frecv_sem.at[slot],
            device_id={"seq": sibling, "chan": chan}, device_id_type=MESH)

    w_own = pltpu.make_async_copy(w_ref.at[:, pl.ds(pl.multiple_of(chan * cols, cols), cols)], wall.at[chan], wown_sem)

    def start_blocks(n):
        @pl.loop(1, seq_count)
        def _(j):
            to = (me + j) % seq_count
            block_copy(n, to, me, to).start()
        recv[n, me] = send[n, me]

    def convolve(n):
        @pl.loop(1, seq_count)
        def _(j):
            source = (me + j) % seq_count
            block_copy(n, source, source, source).wait_recv()

        for g in range(groups):
            staged[g] = recv[n, :, :, g * LANES:(g + 1) * LANES].astype(F32).reshape(seq_count * 2 * per, LANES)

        def gather_rows(row):
            parts = [staged[g, pl.ds(row, seq_count, stride=2 * per)] for g in range(groups)]
            return jnp.concatenate(parts, axis=0)

        def spectrum(row):
            signal = jnp.concatenate((gather_rows(row), gather_rows(row + per)), axis=1).astype(BF16)
            stage = mm(first_ref[...], jnp.concatenate((signal, signal), axis=0))
            cosine = jnp.concatenate((tcos_ref[...], tcos_ref[...]), axis=1)
            sine = jnp.concatenate((tsin_ref[...], tsin_ref[...]), axis=1)
            real, imag = stage[:coarse], stage[coarse:]
            turned_re = real * cosine + imag * sine
            turned_im = imag * cosine - real * sine
            joined = jnp.concatenate((
                jnp.concatenate((turned_re[:, :LANES], turned_im[:, :LANES]), axis=1),
                jnp.concatenate((turned_re[:, LANES:], turned_im[:, LANES:]), axis=1)), axis=0)
            high, low = split(joined)
            both = mm(high, sec_hi[...]) + mm(low, sec_hi[...]) + mm(high, sec_lo[...])
            p_re, p_im = both[:coarse, :LANES], both[:coarse, LANES:]
            h_re, h_im = both[coarse:, :LANES], both[coarse:, LANES:]
            return jnp.concatenate((p_re * h_re - p_im * h_im, p_re * h_im + p_im * h_re), axis=1)

        def pair(step):
            first = 2 * step
            spectra = jnp.concatenate((spectrum(first), spectrum(first + 1)), axis=0)
            high, low = split(spectra)
            back = mm(high, isec_hi[...]) + mm(low, isec_hi[...]) + mm(high, isec_lo[...])
            cosine = jnp.concatenate((tcos_ref[...], tcos_ref[...]), axis=0)
            sine = jnp.concatenate((tsin_ref[...], tsin_ref[...]), axis=0)
            real, imag = back[:, :LANES], back[:, LANES:]
            turned_re = real * cosine - imag * sine
            turned_im = imag * cosine + real * sine
            joined = jnp.concatenate((
                jnp.concatenate((turned_re[:coarse], turned_re[coarse:]), axis=1),
                jnp.concatenate((turned_im[:coarse], turned_im[coarse:]), axis=1)), axis=0)
            high, low = split(joined)
            result = mm(ifirst_hi[...], high) + mm(ifirst_hi[...], low) + mm(ifirst_lo[...], high)
            for c in range(2):
                for g in range(groups):
                    ybuf[g % 2, pl.ds((g // 2) * per + first + c, seq_count, stride=2 * per)] = (
                        result[g * seq_count:(g + 1) * seq_count, c * LANES:(c + 1) * LANES])

        @pl.loop(0, per // 2)
        def _(step):
            pair(step)

        for g in range(2):
            ysend[n, :, :, g * LANES:(g + 1) * LANES] = ybuf[g].astype(BF16).reshape(seq_count, 2 * per, LANES)

        @pl.loop(1, seq_count)
        def _(j):
            to = (me + j) % seq_count
            back_copy(n, to, me, to).start()
        yrecv[n, me] = ysend[n, me]

    def gate(n):
        @pl.loop(1, seq_count)
        def _(j):
            source = (me + j) % seq_count
            back_copy(n, source, source, source).wait_recv()

        cut = slice(n * width, (n + 1) * width)
        unit = eye(rows // 2)
        arrived = yrecv[n].astype(F32).reshape(seq_count, 2, per, rows // 2)
        for part in range(2):
            at = slice(part * (rows // 2), (part + 1) * (rows // 2))
            conv = mm_nt(unit, arrived[:, part].reshape(width, rows // 2).astype(BF16))
            product = k_ref[at, cut].astype(F32) * v_ref[at, cut].astype(F32)
            gated = q_ref[at, cut].astype(F32) * (conv + skip_ref[:, cut] * product)
            gown[n, at] = gated.astype(BF16)

        @pl.loop(1, chan_count)
        def _(j):
            gated_copy(n, chan, (chan + j) % chan_count).start()

    def project(n):
        for j in range(chan_count):
            source = (chan + j) % chan_count
            if j > 0:
                gated_copy(n, source, source).wait_recv()
                left = gall[n, source]
            else:
                left = gown[n]
            term = mm(left, wall[source, n * width:(n + 1) * width])
            if n == 0 and j == 0:
                acc[...] = term
            elif n == CHUNKS - 1 and j == chan_count - 1:
                out_ref[...] = (acc[...] + term).astype(BF16)
            else:
                acc[...] += term

    start_blocks(0)
    prepare(1)
    start_blocks(1)
    w_own.start()

    @pl.loop(1, chan_count)
    def _(j):
        other, seq_to = w_peer(j)
        w_copy(chan, other, seq_to).start()

    convolve(0)
    convolve(1)
    gate(0)

    @pl.loop(1, chan_count)
    def _(j):
        other, seq_to = w_peer(j)
        w_copy(other, other, seq_to).wait_recv()
        w_share(other, core).start()

    gate(1)
    w_own.wait()

    @pl.loop(1, chan_count)
    def _(j):
        other, seq_to = w_peer(j)
        w_share(other, 1 - core).wait_recv()

    project(0)
    project(1)

    @pl.loop(1, seq_count)
    def _(j):
        to = (me + j) % seq_count
        for n in range(CHUNKS):
            block_copy(n, to, to, to).wait_send()
            back_copy(n, to, to, to).wait_send()

    @pl.loop(1, chan_count)
    def _(j):
        other, seq_to = w_peer(j)
        for n in range(CHUNKS):
            gated_copy(n, other, other).wait_send()
        w_copy(other, other, seq_to).wait_send()
        w_share(other, core).wait_send()


def on_device(seq_count, chan_count, query_rows, key_rows, value_rows, filter_taps, skip_gain, w_out):
    rows, channels = query_rows.shape
    cols = w_out.shape[1] // chan_count
    width = channels // CHUNKS
    per = width // seq_count
    tables = [jnp.asarray(t) for t in transform_tables(seq_count, rows // LANES)]
    vmem = pl.BlockSpec(memory_space=pltpu.VMEM)
    dma = pltpu.SemaphoreType.DMA
    return pl.pallas_call(
        functools.partial(kernel, seq_count, chan_count),
        out_shape=jax.ShapeDtypeStruct((rows, cols), BF16),
        in_specs=[vmem] * 5 + [pl.BlockSpec(memory_space=pl.ANY)] + [vmem] * len(tables),
        out_specs=vmem,
        scratch_shapes=[
            pltpu.VMEM((CHUNKS, seq_count, 2 * per, rows), BF16),
            pltpu.VMEM((CHUNKS, seq_count, 2 * per, rows), BF16),
            pltpu.VMEM((rows // LANES, seq_count * 2 * per, LANES), F32),
            pltpu.VMEM((CHUNKS, seq_count, 2 * per, rows // 2), BF16),
            pltpu.VMEM((CHUNKS, seq_count, 2 * per, rows // 2), BF16),
            pltpu.VMEM((2, seq_count * 2 * per, LANES), F32),
            pltpu.VMEM((CHUNKS, rows, width), BF16),
            pltpu.VMEM((CHUNKS, chan_count, rows, width), BF16),
            pltpu.VMEM((chan_count, channels, cols), BF16),
            pltpu.VMEM((rows, cols), F32),
            dma((CHUNKS, seq_count)), dma((CHUNKS, seq_count)),
            dma((CHUNKS, seq_count)), dma((CHUNKS, seq_count)),
            dma((CHUNKS, chan_count)), dma((CHUNKS, chan_count)),
            dma((chan_count,)), dma((chan_count,)), dma((chan_count,)), dma((chan_count,)),
            dma,
        ],
        compiler_params=pltpu.CompilerParams(
            collective_id=0, has_side_effects=True, vmem_limit_bytes=56 * 1024 * 1024),
    )(query_rows, key_rows, value_rows, filter_taps, skip_gain.reshape(1, channels), w_out, *tables)


def solution(mesh):
    return jax.shard_map(
        functools.partial(on_device, mesh.shape["seq"], mesh.shape["chan"]),
        mesh=mesh,
        in_specs=(
            P("seq", "chan"),
            P("seq", "chan"),
            P("seq", "chan"),
            P("seq", "chan"),
            P("chan"),
            P("chan", None),
        ),
        out_specs=P("seq", "chan"),
        check_vma=False,
    )
```

time: 749 us -> 161 us (0.21)
  the two profiles are of different devices: /device:TPU:2 before, /device:TPU:22 now
where the time goes in v1:
time: 161 us
  Pallas kernels  159 us (99%)
  local copies, waits for them, and re-layouts  2.26 us (1%)
    pallas_call x1, Pallas kernels, on_device(): pl.pallas_call(functools.partial(kernel, seq_count, chan_count), out_shap...  159 us

profile of v1, /device:TPU:22, one launch (start us, length us, event | category | flops | bytes accessed | tf_op | source)
XLA Modules:
  0.0 161.4 jit_solution(2378959298485888732)
XLA Ops:
  0.0 159.1 %shard_map.145 = bf16[512,1024]{1,0:T(8,128)(2,1)} custom-call(bf16[512,512]{1,0:T(8,128)(2,1)} %q_ref.1, bf16[512,512]{1,0:T(8,128)(2,1)} %k_ref.1, bf16[512,512]{1,0:T(8,128)(2,1)} %v_ref.1, f32[512,512]{1,0:T(8,128)} %h_ref.1, f32[1,512]{1,0:T(1,128)} %bitcast.1, bf16[512,8192]{1,0:T(8,128)(2,1)} %w_ref.1, bf16[256,256]{1,0:T(8,128)(2,1)} %constant.18.clone.first_ref, ...), custom_call_target="tpu_custom_call" | custom-call | tf_op jit(solution)/shard_map/pallas_call | solution.py:323
  159.1 2.3 %copy.17 = bf16[512,1024]{1,0:T(8,128)(2,1)} copy(bf16[512,1024]{1,0:T(8,128)(2,1)} %shard_map.145) | data formatting | bytes 2097152

commit v2 on v1

--- a/solution.py
+++ b/solution.py
@@ -73,8 +73,8 @@
     q_ref, k_ref, v_ref, h_ref, skip_ref, w_ref,
     first_ref, tcos_ref, tsin_ref, sec_hi, sec_lo, isec_hi, isec_lo, ifirst_hi, ifirst_lo,
     out_ref,
-    send, recv, staged, ysend, yrecv, ybuf, gown, gall, wall, acc,
-    send_sem, recv_sem, ysend_sem, yrecv_sem, gsend_sem, grecv_sem,
+    send, recv, staged, ysend, yrecv, ybuf, gall, wall, acc, psend, precv,
+    send_sem, recv_sem, ysend_sem, yrecv_sem, gsend_sem, grecv_sem, psend_sem, precv_sem,
     wsend_sem, wrecv_sem, fsend_sem, frecv_sem, wown_sem,
 ):
     rows, channels = q_ref.shape
@@ -83,34 +83,38 @@
     per = width // seq_count
     coarse = seq_count * groups
     cols = out_ref.shape[1]
-    half_rows = channels // 2
     y_count = chan_count // 2
+    half = rows // 2
     me = lax.axis_index("seq")
     chan = lax.axis_index("chan")
     core = me % 2
-    flipped = me + 2 - 4 * ((me // 2) % 2)
+    x_lo = (me // 2) % 2
+    parity = (me // 4) % 2
+    sibling = me + 1 - 2 * core
+    mate = me + 2 - 4 * x_lo
+    above = (me + 4) % seq_count
+    below = (me + seq_count - 4) % seq_count
     x_hi = chan // y_count
-    sibling = me + 1 - 2 * core
-
-    def w_peer(j):
-        other = (chan + j) % chan_count
-        seq_to = jnp.where(other // y_count == x_hi, me, flipped)
-        return other, seq_to
+    y = chan % y_count
+    facing = (1 - x_hi) * y_count + y
+
+    def y_peer(j):
+        return (y + j) % y_count
+
+    def device(seq_to, chan_to):
+        return {"seq": seq_to, "chan": chan_to}
 
     barrier = pltpu.get_barrier_semaphore()
 
     @pl.loop(1, seq_count)
     def _(j):
-        pl.semaphore_signal(barrier, inc=1, device_id={"seq": (me + j) % seq_count, "chan": chan}, device_id_type=MESH)
-
-    @pl.loop(1, chan_count)
+        pl.semaphore_signal(barrier, inc=1, device_id=device((me + j) % seq_count, chan), device_id_type=MESH)
+
+    @pl.loop(1, y_count)
     def _(j):
-        pl.semaphore_signal(barrier, inc=1, device_id={"seq": me, "chan": (chan + j) % chan_count}, device_id_type=MESH)
-
-    @pl.loop(0, y_count)
-    def _(j):
-        other = ((1 - x_hi) * y_count) + j
-        pl.semaphore_signal(barrier, inc=1, device_id={"seq": flipped, "chan": other}, device_id_type=MESH)
+        pl.semaphore_signal(barrier, inc=1, device_id=device(me, x_hi * y_count + y_peer(j)), device_id_type=MESH)
+
+    pl.semaphore_signal(barrier, inc=1, device_id=device(me, facing), device_id_type=MESH)
 
     def prepare(n):
         cut = slice(n * width, (n + 1) * width)
@@ -121,7 +125,7 @@
         send[n] = jnp.concatenate((p_rows, h_rows), axis=1).astype(BF16)
 
     prepare(0)
-    pl.semaphore_wait(barrier, seq_count - 1 + chan_count - 1 + y_count)
+    pl.semaphore_wait(barrier, seq_count + y_count - 1)
 
     def block_copy(n, slot_out, slot_in, to):
         return pltpu.make_async_remote_copy(
@@ -135,29 +139,112 @@
             send_sem=ysend_sem.at[n, slot_out], recv_sem=yrecv_sem.at[n, slot_in],
             device_id={"seq": to, "chan": chan}, device_id_type=MESH)
 
-    def gated_copy(n, slot_in, other):
-        return pltpu.make_async_remote_copy(
-            src_ref=gown.at[n], dst_ref=gall.at[n, slot_in],
-            send_sem=gsend_sem.at[n, other], recv_sem=grecv_sem.at[n, slot_in],
-            device_id={"seq": me, "chan": other}, device_id_type=MESH)
-
-    own_half = pl.ds(pl.multiple_of(core * half_rows, half_rows), half_rows)
-
-    def w_copy(slot_in, other, seq_to):
-        return pltpu.make_async_remote_copy(
-            src_ref=w_ref.at[own_half, pl.ds(pl.multiple_of(other * cols, cols), cols)],
-            dst_ref=wall.at[slot_in, own_half],
-            send_sem=wsend_sem.at[other], recv_sem=wrecv_sem.at[slot_in],
-            device_id={"seq": seq_to, "chan": other}, device_id_type=MESH)
-
-    def w_share(slot, half):
-        part = pl.ds(pl.multiple_of(half * half_rows, half_rows), half_rows)
-        return pltpu.make_async_remote_copy(
-            src_ref=wall.at[slot, part], dst_ref=wall.at[slot, part],
-            send_sem=fsend_sem.at[slot], recv_sem=frecv_sem.at[slot],
-            device_id={"seq": sibling, "chan": chan}, device_id_type=MESH)
-
-    w_own = pltpu.make_async_copy(w_ref.at[:, pl.ds(pl.multiple_of(chan * cols, cols), cols)], wall.at[chan], wown_sem)
+    def gated_copy(n, part, slot, to):
+        lanes = pl.ds(pl.multiple_of(slot * width, width), width)
+        block = gall.at[n, pl.ds(part * half, half), lanes]
+        return pltpu.make_async_remote_copy(
+            src_ref=block, dst_ref=block,
+            send_sem=gsend_sem.at[n, part, to], recv_sem=grecv_sem.at[n, part, slot],
+            device_id=device(me, x_hi * y_count + to), device_id_type=MESH)
+
+    def partial_copy(part):
+        at = pl.ds(part * half, half)
+        return pltpu.make_async_remote_copy(
+            src_ref=psend.at[at], dst_ref=precv.at[at],
+            send_sem=psend_sem.at[part], recv_sem=precv_sem.at[part],
+            device_id=device(me, facing), device_id_type=MESH)
+
+    core_rows = width // 2
+    direct, by_pair, by_level = width // 8, width // 16, width // 8
+    pair_base = direct
+    level_base = direct + 2 * by_pair
+    classes = (
+        (direct, lambda: core * core_rows),
+        (by_pair, lambda: core * core_rows + pair_base + x_lo * by_pair),
+        (by_level, lambda: core * core_rows + level_base + parity * by_level),
+    )
+
+    def some_rows(start, size):
+        return pl.ds(pl.multiple_of(start, 16), size)
+
+    def side_of(col_side, x_side, y_side):
+        target = jnp.where(col_side == 0, x_side, 1 - x_side)
+        return pl.ds(pl.multiple_of((target * y_count + y_side) * cols, cols), cols)
+
+    def w_copy(kind, col_side, slot, to):
+        size, start = classes[kind]
+        return pltpu.make_async_remote_copy(
+            src_ref=w_ref.at[:, some_rows(start(), size), side_of(col_side, x_hi, to)],
+            dst_ref=wall.at[:, slot, some_rows(start(), size), pl.ds(col_side * cols, cols)],
+            send_sem=wsend_sem.at[kind, col_side, to], recv_sem=wrecv_sem.at[kind, col_side, slot],
+            device_id=device(me, x_hi * y_count + to), device_id_type=MESH)
+
+    def w_pass(route, slot, start, size, seq_to):
+        block = wall.at[:, slot, some_rows(start, size)]
+        return pltpu.make_async_remote_copy(
+            src_ref=block, dst_ref=block,
+            send_sem=fsend_sem.at[route, slot], recv_sem=frecv_sem.at[route, slot],
+            device_id=device(seq_to, chan), device_id_type=MESH)
+
+    def pass_pair(slot, x_side):
+        return w_pass(0, slot, core * core_rows + pair_base + x_side * by_pair, by_pair, mate)
+
+    def pass_level(up, slot, level_side):
+        size = by_level // 2
+        start = core * core_rows + level_base + level_side * by_level + (0 if up else size)
+        return w_pass(1 if up else 2, slot, start, size, above if up else below)
+
+    def pass_core(slot, side):
+        return w_pass(3, slot, side * core_rows, core_rows, sibling)
+
+    def own_copy(col_side):
+        return pltpu.make_async_copy(
+            w_ref.at[:, :, side_of(col_side, x_hi, y)],
+            wall.at[:, y, :, pl.ds(col_side * cols, cols)], wown_sem.at[col_side])
+
+    def start_w(kind):
+        @pl.loop(1, y_count)
+        def _(j):
+            for col_side in range(2):
+                w_copy(kind, col_side, y, y_peer(j)).start()
+
+    def wait_w(kind):
+        @pl.loop(1, y_count)
+        def _(j):
+            for col_side in range(2):
+                w_copy(kind, col_side, y_peer(j), y_peer(j)).wait_recv()
+
+    def share_w():
+        wait_w(1)
+
+        @pl.loop(1, y_count)
+        def _(j):
+            pass_pair(y_peer(j), x_lo).start()
+
+        wait_w(2)
+
+        @pl.loop(1, y_count)
+        def _(j):
+            pass_level(True, y_peer(j), parity).start()
+            pass_level(False, y_peer(j), parity).start()
+
+    def finish_w():
+        wait_w(0)
+
+        @pl.loop(1, y_count)
+        def _(j):
+            slot = y_peer(j)
+            pass_pair(slot, 1 - x_lo).wait_recv()
+            pass_level(True, slot, 1 - parity).wait_recv()
+            pass_level(False, slot, 1 - parity).wait_recv()
+            pass_core(slot, core).start()
+
+        own_copy(0).wait()
+        own_copy(1).wait()
+
+        @pl.loop(1, y_count)
+        def _(j):
+            pass_core(y_peer(j), 1 - core).wait_recv()
 
     def start_blocks(n):
         @pl.loop(1, seq_count)
@@ -236,65 +323,83 @@
             back_copy(n, source, source, source).wait_recv()
 
         cut = slice(n * width, (n + 1) * width)
-        unit = eye(rows // 2)
-        arrived = yrecv[n].astype(F32).reshape(seq_count, 2, per, rows // 2)
+        unit = eye(half)
+        arrived = yrecv[n].astype(F32).reshape(seq_count, 2, per, half)
+        lanes = pl.ds(pl.multiple_of(y * width, width), width)
         for part in range(2):
-            at = slice(part * (rows // 2), (part + 1) * (rows // 2))
-            conv = mm_nt(unit, arrived[:, part].reshape(width, rows // 2).astype(BF16))
+            at = slice(part * half, (part + 1) * half)
+            conv = mm_nt(unit, arrived[:, part].reshape(width, half).astype(BF16))
             product = k_ref[at, cut].astype(F32) * v_ref[at, cut].astype(F32)
             gated = q_ref[at, cut].astype(F32) * (conv + skip_ref[:, cut] * product)
-            gown[n, at] = gated.astype(BF16)
-
-        @pl.loop(1, chan_count)
-        def _(j):
-            gated_copy(n, chan, (chan + j) % chan_count).start()
-
-    def project(n):
-        for j in range(chan_count):
-            source = (chan + j) % chan_count
-            if j > 0:
-                gated_copy(n, source, source).wait_recv()
-                left = gall[n, source]
-            else:
-                left = gown[n]
-            term = mm(left, wall[source, n * width:(n + 1) * width])
-            if n == 0 and j == 0:
-                acc[...] = term
-            elif n == CHUNKS - 1 and j == chan_count - 1:
-                out_ref[...] = (acc[...] + term).astype(BF16)
-            else:
-                acc[...] += term
+            gall[n, at, lanes] = gated.astype(BF16)
+
+        @pl.loop(1, y_count)
+        def _(j):
+            for part in range(2):
+                gated_copy(n, part, y, y_peer(j)).start()
+
+    def wait_gated(n, part):
+        @pl.loop(1, y_count)
+        def _(j):
+            gated_copy(n, part, y_peer(j), y_peer(j)).wait_recv()
+
+    tile = min(cols, 512)
+    tiles = cols // tile
+
+    def term(n, part, lanes):
+        at = slice(part * half, (part + 1) * half)
+        return mm(gall[n, at], wall[n, :, :, lanes].reshape(y_count * width, tile))
+
+    def tile_at(side, step):
+        return pl.ds(pl.multiple_of(side * cols + step * tile, tile), tile)
+
+    def project_first():
+        for part in range(2):
+            wait_gated(0, part)
+
+            @pl.loop(0, 2 * tiles)
+            def _(step):
+                acc[part * half:(part + 1) * half, tile_at(0, step)] = term(0, part, tile_at(0, step))
+
+    def project_last():
+        for part in range(2):
+            at = slice(part * half, (part + 1) * half)
+            wait_gated(1, part)
+
+            @pl.loop(0, tiles)
+            def _(step):
+                psend[at, tile_at(0, step)] = (acc[at, tile_at(1, step)] + term(1, part, tile_at(1, step))).astype(BF16)
+
+            partial_copy(part).start()
+
+        for part in range(2):
+            at = slice(part * half, (part + 1) * half)
+
+            @pl.loop(0, tiles)
+            def _(step):
+                acc[at, tile_at(0, step)] += term(1, part, tile_at(0, step))
+
+        for part in range(2):
+            at = slice(part * half, (part + 1) * half)
+            partial_copy(part).wait_recv()
+            out_ref[at] = (acc[at, :cols] + precv[at].astype(F32)).astype(BF16)
 
     start_blocks(0)
     prepare(1)
     start_blocks(1)
-    w_own.start()
-
-    @pl.loop(1, chan_count)
-    def _(j):
-        other, seq_to = w_peer(j)
-        w_copy(chan, other, seq_to).start()
-
+    start_w(2)
+    start_w(1)
+    start_w(0)
+    own_copy(0).start()
+    own_copy(1).start()
     convolve(0)
     convolve(1)
+    share_w()
     gate(0)
-
-    @pl.loop(1, chan_count)
-    def _(j):
-        other, seq_to = w_peer(j)
-        w_copy(other, other, seq_to).wait_recv()
-        w_share(other, core).start()
-
     gate(1)
-    w_own.wait()
-
-    @pl.loop(1, chan_count)
-    def _(j):
-        other, seq_to = w_peer(j)
-        w_share(other, 1 - core).wait_recv()
-
-    project(0)
-    project(1)
+    finish_w()
+    project_first()
+    project_last()
 
     @pl.loop(1, seq_count)
     def _(j):
@@ -303,13 +408,22 @@
             block_copy(n, to, to, to).wait_send()
             back_copy(n, to, to, to).wait_send()
 
-    @pl.loop(1, chan_count)
+    @pl.loop(1, y_count)
     def _(j):
-        other, seq_to = w_peer(j)
+        slot = y_peer(j)
         for n in range(CHUNKS):
-            gated_copy(n, other, other).wait_send()
-        w_copy(other, other, seq_to).wait_send()
-        w_share(other, core).wait_send()
+            for part in range(2):
+                gated_copy(n, part, y, slot).wait_send()
+        for kind in range(3):
+            for col_side in range(2):
+                w_copy(kind, col_side, y, slot).wait_send()
+        pass_pair(slot, x_lo).wait_send()
+        pass_level(True, slot, parity).wait_send()
+        pass_level(False, slot, parity).wait_send()
+        pass_core(slot, core).wait_send()
+
+    for part in range(2):
+        partial_copy(part).wait_send()
 
 
 def on_device(seq_count, chan_count, query_rows, key_rows, value_rows, filter_taps, skip_gain, w_out):
@@ -317,6 +431,7 @@
     cols = w_out.shape[1] // chan_count
     width = channels // CHUNKS
     per = width // seq_count
+    y_count = chan_count // 2
     tables = [jnp.asarray(t) for t in transform_tables(seq_count, rows // LANES)]
     vmem = pl.BlockSpec(memory_space=pltpu.VMEM)
     dma = pltpu.SemaphoreType.DMA
@@ -332,19 +447,23 @@
             pltpu.VMEM((CHUNKS, seq_count, 2 * per, rows // 2), BF16),
             pltpu.VMEM((CHUNKS, seq_count, 2 * per, rows // 2), BF16),
             pltpu.VMEM((2, seq_count * 2 * per, LANES), F32),
-            pltpu.VMEM((CHUNKS, rows, width), BF16),
-            pltpu.VMEM((CHUNKS, chan_count, rows, width), BF16),
-            pltpu.VMEM((chan_count, channels, cols), BF16),
-            pltpu.VMEM((rows, cols), F32),
+            pltpu.VMEM((CHUNKS, rows, y_count * width), BF16),
+            pltpu.VMEM((CHUNKS, y_count, width, 2 * cols), BF16),
+            pltpu.VMEM((rows, 2 * cols), F32),
+            pltpu.VMEM((rows, cols), BF16),
+            pltpu.VMEM((rows, cols), BF16),
             dma((CHUNKS, seq_count)), dma((CHUNKS, seq_count)),
             dma((CHUNKS, seq_count)), dma((CHUNKS, seq_count)),
-            dma((CHUNKS, chan_count)), dma((CHUNKS, chan_count)),
-            dma((chan_count,)), dma((chan_count,)), dma((chan_count,)), dma((chan_count,)),
-            dma,
+            dma((CHUNKS, 2, y_count)), dma((CHUNKS, 2, y_count)),
+            dma((2,)), dma((2,)),
+            dma((3, 2, y_count)), dma((3, 2, y_count)),
+            dma((4, y_count)), dma((4, y_count)),
+            dma((2,)),
         ],
         compiler_params=pltpu.CompilerParams(
             collective_id=0, has_side_effects=True, vmem_limit_bytes=56 * 1024 * 1024),
-    )(query_rows, key_rows, value_rows, filter_taps, skip_gain.reshape(1, channels), w_out, *tables)
+    )(query_rows, key_rows, value_rows, filter_taps, skip_gain.reshape(1, channels),
+      w_out.reshape(CHUNKS, width, w_out.shape[1]), *tables)
 
 
 def solution(mesh):

time: 161 us -> 99.7 us (0.62)
  the two profiles are of different devices: /device:TPU:22 before, /device:TPU:2 now
where the time goes in v2:
time: 99.7 us; the launch traced here: 99.5 us
  Pallas kernels  97.3 us (98%)
  local copies, waits for them, and re-layouts  2.26 us (2%)
    pallas_call x1, Pallas kernels, on_device(): pl.pallas_call(functools.partial(kernel, seq_count, chan_count), out_shap...  97.3 us
    unnamed x1, local copies, waits for them, and re-layouts  2.26 us

profile of v2, /device:TPU:2, one launch (start us, length us, event | category | flops | bytes accessed | tf_op | source)
XLA Modules:
  0.0 99.5 jit_solution(6113797947876608983)
XLA Ops:
  0.0 97.3 %shard_map.145 = bf16[512,1024]{1,0:T(8,128)(2,1)} custom-call(bf16[512,512]{1,0:T(8,128)(2,1)} %q_ref.1, bf16[512,512]{1,0:T(8,128)(2,1)} %k_ref.1, bf16[512,512]{1,0:T(8,128)(2,1)} %v_ref.1, f32[512,512]{1,0:T(8,128)} %h_ref.1, f32[1,512]{1,0:T(1,128)} %bitcast.3, bf16[2,256,8192]{2,1,0:T(8,128)(2,1)} %bitcast.2, ...), custom_call_target="tpu_custom_call" | custom-call | tf_op jit(solution)/shard_map/pallas_call | solution.py:438
  97.3 2.3 %copy.17 = bf16[512,1024]{1,0:T(8,128)(2,1)} copy(bf16[512,1024]{1,0:T(8,128)(2,1)} %shard_map.145) | data formatting | bytes 2097152

commit v3 on v2

v3 whole, which is shorter than its diff:
```python
import functools

import jax
import jax.numpy as jnp
import ml_dtypes
import numpy as np
from jax import lax
from jax.experimental import pallas as pl
from jax.experimental.pallas import tpu as pltpu
from jax.sharding import PartitionSpec as P

MESH = pl.DeviceIdType.MESH
LANES = 128
CHUNKS = 2
PARTS = 4
BF16 = jnp.bfloat16
F32 = jnp.float32


def split_table(table):
    high = table.astype(ml_dtypes.bfloat16)
    low = (table - high.astype(np.float64)).astype(ml_dtypes.bfloat16)
    return high, low


def transform_tables(seq_count, row_groups):
    coarse = seq_count * row_groups
    total = coarse * LANES
    freq = np.arange(coarse) + 0.25
    order = (np.arange(seq_count)[None, :] * row_groups + np.arange(row_groups)[:, None]).reshape(-1)
    angle = 2.0 * np.pi * freq[:, None] * order[None, :] / coarse
    forward_first = np.concatenate((np.cos(angle), -np.sin(angle)), axis=0)
    inverse_first = np.concatenate((np.cos(angle).T, -np.sin(angle).T), axis=1) / total
    fine = np.arange(LANES)
    turn = 2.0 * np.pi * freq[:, None] * fine[None, :] / total
    twist_cos = np.cos(turn).astype(np.float32)
    twist_sin = np.sin(turn).astype(np.float32)
    inner = 2.0 * np.pi * (fine[:, None] * fine[None, :] % LANES) / LANES
    cosine, sine = np.cos(inner), np.sin(inner)
    forward_second = np.block([[cosine, -sine], [sine, cosine]])
    inverse_second = np.block([[cosine, sine], [-sine, cosine]])
    turns = np.stack((twist_cos, twist_sin))
    inner = np.stack((*split_table(forward_second), *split_table(inverse_second)))
    first = np.concatenate(split_table(forward_first), axis=1)
    last = np.stack(split_table(inverse_first))
    return turns, inner, first, last


def mm(left, right):
    return jnp.dot(left, right, preferred_element_type=F32)


def mm_nt(left, right):
    return lax.dot_general(left, right, (((1,), (1,)), ((), ())), preferred_element_type=F32)


def split(value):
    high = value.astype(BF16)
    low = (value - high.astype(F32)).astype(BF16)
    return high, low


def eye(size):
    row = lax.broadcasted_iota(jnp.int32, (size, size), 0)
    col = lax.broadcasted_iota(jnp.int32, (size, size), 1)
    return (row == col).astype(F32).astype(BF16)


def kernel(
    seq_count, chan_count,
    q_hbm, k_hbm, v_hbm, h_hbm, skip_hbm, w_ref, turns_hbm, inner_hbm, first_hbm, last_hbm,
    own_ref, precv,
    q_ref, k_ref, v_ref, h_ref, skip_ref, turns_ref, inner_ref, first_ref, last_ref, load_sem,
    send, recv, staged, ysend, yrecv, ybuf, gall, wall, acc, psend,
    send_sem, recv_sem, ysend_sem, yrecv_sem, gsend_sem, grecv_sem, psend_sem, precv_sem,
    wsend_sem, wrecv_sem, fsend_sem, frecv_sem, wown_sem, own_sem,
):
    rows, channels = q_ref.shape
    groups = rows // LANES
    width = channels // CHUNKS
    per = width // seq_count
    coarse = seq_count * groups
    cols = own_ref.shape[1]
    y_count = chan_count // 2
    half = rows // 2
    part_rows = rows // PARTS
    me = lax.axis_index("seq")
    chan = lax.axis_index("chan")
    core = me % 2
    x_lo = (me // 2) % 2
    sibling = me + 1 - 2 * core
    mate = me + 2 - 4 * x_lo
    x_hi = chan // y_count
    y = chan % y_count
    facing = (1 - x_hi) * y_count + y

    def y_peer(j):
        return (y + j) % y_count

    def device(seq_to, chan_to):
        return {"seq": seq_to, "chan": chan_to}

    barrier = pltpu.get_barrier_semaphore()

    @pl.loop(1, seq_count)
    def _(j):
        pl.semaphore_signal(barrier, inc=1, device_id=device((me + j) % seq_count, chan), device_id_type=MESH)

    @pl.loop(1, y_count)
    def _(j):
        pl.semaphore_signal(barrier, inc=1, device_id=device(me, x_hi * y_count + y_peer(j)), device_id_type=MESH)

    pl.semaphore_signal(barrier, inc=1, device_id=device(me, facing), device_id_type=MESH)

    loads = [pltpu.make_async_copy(source, target, load_sem.at[i]) for i, (source, target) in enumerate((
        (k_hbm, k_ref), (v_hbm, v_ref), (h_hbm, h_ref), (turns_hbm, turns_ref), (inner_hbm, inner_ref),
        (first_hbm, first_ref), (last_hbm, last_ref), (q_hbm, q_ref), (skip_hbm, skip_ref)))]
    for load in loads:
        load.start()
    for load in loads[:3]:
        load.wait()

    def prepare(n):
        cut = slice(n * width, (n + 1) * width)
        unit = eye(width)
        product = (k_ref[:, cut].astype(F32) * v_ref[:, cut].astype(F32)).astype(BF16)
        p_rows = mm_nt(unit, product).reshape(seq_count, per, rows)
        h_rows = mm_nt(unit, h_ref[:, cut].astype(BF16)).reshape(seq_count, per, rows)
        send[n] = jnp.concatenate((p_rows, h_rows), axis=1).astype(BF16)

    prepare(0)
    pl.semaphore_wait(barrier, seq_count + y_count - 1)

    def block_copy(n, slot_out, slot_in, to):
        return pltpu.make_async_remote_copy(
            src_ref=send.at[n, slot_out], dst_ref=recv.at[n, slot_in],
            send_sem=send_sem.at[n], recv_sem=recv_sem.at[n],
            device_id={"seq": to, "chan": chan}, device_id_type=MESH)

    def back_copy(n, slot_out, slot_in, to):
        return pltpu.make_async_remote_copy(
            src_ref=ysend.at[n, slot_out], dst_ref=yrecv.at[n, slot_in],
            send_sem=ysend_sem.at[n], recv_sem=yrecv_sem.at[n],
            device_id={"seq": to, "chan": chan}, device_id_type=MESH)

    def gated_copy(n, part, lanes, to):
        block = gall.at[n, pl.ds(part * part_rows, part_rows), lanes]
        return pltpu.make_async_remote_copy(
            src_ref=block, dst_ref=block,
            send_sem=gsend_sem.at[n, part], recv_sem=grecv_sem.at[n, part],
            device_id=device(me, x_hi * y_count + to), device_id_type=MESH)

    def all_gated(n, part):
        return gated_copy(n, part, pl.ds(0, (y_count - 1) * width), y)

    def partial_copy(part):
        at = pl.ds(part * part_rows, part_rows)
        return pltpu.make_async_remote_copy(
            src_ref=psend.at[at], dst_ref=precv.at[at],
            send_sem=psend_sem.at[part], recv_sem=precv_sem.at[part],
            device_id=device(me, facing), device_id_type=MESH)

    core_rows = width // 2
    direct, by_pair = width // 4, width // 8
    pair_base = direct

    def some_rows(start, size):
        return pl.ds(pl.multiple_of(start, 16), size)

    def side_of(col_side, x_side, y_side):
        target = jnp.where(col_side == 0, x_side, 1 - x_side)
        return pl.ds(pl.multiple_of((target * y_count + y_side) * cols, cols), cols)

    def w_copy(kind, col_side, to):
        size = (direct, by_pair)[kind]
        start = core * core_rows + (0, pair_base + x_lo * by_pair)[kind]
        return pltpu.make_async_remote_copy(
            src_ref=w_ref.at[:, some_rows(start, size), side_of(col_side, x_hi, to)],
            dst_ref=wall.at[:, y, some_rows(start, size), pl.ds(col_side * cols, cols)],
            send_sem=wsend_sem.at[kind], recv_sem=wrecv_sem.at[kind],
            device_id=device(me, x_hi * y_count + to), device_id_type=MESH)

    def all_w(kind):
        size = (direct, by_pair)[kind]
        block = wall.at[:, pl.ds(0, y_count - 1), pl.ds(0, size)]
        return pltpu.make_async_remote_copy(
            src_ref=block, dst_ref=block, send_sem=wsend_sem.at[kind], recv_sem=wrecv_sem.at[kind],
            device_id=device(me, facing), device_id_type=MESH)

    def w_pass(route, slot, start, size, seq_to):
        block = wall.at[:, slot, some_rows(start, size)]
        return pltpu.make_async_remote_copy(
            src_ref=block, dst_ref=block, send_sem=fsend_sem.at[route], recv_sem=frecv_sem.at[route],
            device_id=device(seq_to, chan), device_id_type=MESH)

    def pass_pair(slot):
        return w_pass(0, slot, core * core_rows + pair_base + x_lo * by_pair, by_pair, mate)

    def pass_core(slot):
        return w_pass(1, slot, core * core_rows, core_rows, sibling)

    def all_pass(route):
        block = wall.at[:, pl.ds(0, y_count - 1), pl.ds(0, (by_pair, core_rows)[route])]
        return pltpu.make_async_remote_copy(
            src_ref=block, dst_ref=block, send_sem=fsend_sem.at[route], recv_sem=frecv_sem.at[route],
            device_id=device((mate, sibling)[route], chan), device_id_type=MESH)

    def own_copy(col_side):
        return pltpu.make_async_copy(
            w_ref.at[:, :, side_of(col_side, x_hi, y)],
            wall.at[:, y, :, pl.ds(col_side * cols, cols)], wown_sem.at[col_side])

    def start_w(kind):
        @pl.loop(1, y_count)
        def _(j):
            for col_side in range(2):
                w_copy(kind, col_side, y_peer(j)).start()

    def share_w():
        all_w(1).wait_recv()

        @pl.loop(1, y_count)
        def _(j):
            pass_pair(y_peer(j)).start()

    def finish_w():
        all_w(0).wait_recv()
        all_pass(0).wait_recv()

        @pl.loop(1, y_count)
        def _(j):
            pass_core(y_peer(j)).start()

        own_copy(0).wait()
        own_copy(1).wait()
        all_pass(1).wait_recv()

    def start_blocks(n):
        @pl.loop(1, seq_count)
        def _(j):
            to = (me + j) % seq_count
            block_copy(n, to, me, to).start()
        recv[n, me] = send[n, me]

    others = pl.ds(0, seq_count - 1)

    def all_blocks(n):
        return block_copy(n, others, others, me)

    def all_back(n):
        return back_copy(n, others, others, me)

    def convolve(n, between=None):
        all_blocks(n).wait_recv()

        for g in range(groups):
            staged[g] = recv[n, :, :, g * LANES:(g + 1) * LANES].astype(F32).reshape(seq_count * 2 * per, LANES)

        def gather_rows(row):
            parts = [staged[g, pl.ds(row, seq_count, stride=2 * per)] for g in range(groups)]
            return jnp.concatenate(parts, axis=0)

        def spectrum(row):
            signal = jnp.concatenate((gather_rows(row), gather_rows(row + per)), axis=1).astype(BF16)
            stage = mm(first_ref[...], jnp.concatenate((signal, signal), axis=0))
            cosine = jnp.concatenate((turns_ref[0], turns_ref[0]), axis=1)
            sine = jnp.concatenate((turns_ref[1], turns_ref[1]), axis=1)
            real, imag = stage[:coarse], stage[coarse:]
            turned_re = real * cosine + imag * sine
            turned_im = imag * cosine - real * sine
            joined = jnp.concatenate((
                jnp.concatenate((turned_re[:, :LANES], turned_im[:, :LANES]), axis=1),
                jnp.concatenate((turned_re[:, LANES:], turned_im[:, LANES:]), axis=1)), axis=0)
            high, low = split(joined)
            both = mm(high, inner_ref[0]) + mm(low, inner_ref[0]) + mm(high, inner_ref[1])
            p_re, p_im = both[:coarse, :LANES], both[:coarse, LANES:]
            h_re, h_im = both[coarse:, :LANES], both[coarse:, LANES:]
            return jnp.concatenate((p_re * h_re - p_im * h_im, p_re * h_im + p_im * h_re), axis=1)

        def pair(step):
            first = 2 * step
            spectra = jnp.concatenate((spectrum(first), spectrum(first + 1)), axis=0)
            high, low = split(spectra)
            back = mm(high, inner_ref[2]) + mm(low, inner_ref[2]) + mm(high, inner_ref[3])
            cosine = jnp.concatenate((turns_ref[0], turns_ref[0]), axis=0)
            sine = jnp.concatenate((turns_ref[1], turns_ref[1]), axis=0)
            real, imag = back[:, :LANES], back[:, LANES:]
            turned_re = real * cosine - imag * sine
            turned_im = imag * cosine + real * sine
            joined = jnp.concatenate((
                jnp.concatenate((turned_re[:coarse], turned_re[coarse:]), axis=1),
                jnp.concatenate((turned_im[:coarse], turned_im[coarse:]), axis=1)), axis=0)
            high, low = split(joined)
            result = mm(last_ref[0], high) + mm(last_ref[0], low) + mm(last_ref[1], high)
            for c in range(2):
                for g in range(groups):
                    ybuf[g % 2, pl.ds((g // 2) * per + first + c, seq_count, stride=2 * per)] = (
                        result[g * seq_count:(g + 1) * seq_count, c * LANES:(c + 1) * LANES])

        steps = per // 2
        for step in range(steps):
            if between is not None and step == steps // 2:
                between()
            pair(step)

        for g in range(2):
            ysend[n, :, :, g * LANES:(g + 1) * LANES] = ybuf[g].astype(BF16).reshape(seq_count, 2 * per, LANES)

        @pl.loop(1, seq_count)
        def _(j):
            to = (me + j) % seq_count
            back_copy(n, to, me, to).start()
        yrecv[n, me] = ysend[n, me]

    def gate(n):
        all_back(n).wait_recv()

        cut = slice(n * width, (n + 1) * width)
        unit = eye(half)
        arrived = yrecv[n].astype(F32).reshape(seq_count, 2, per, half)
        lanes = pl.ds(pl.multiple_of(y * width, width), width)
        for part in range(2):
            at = slice(part * half, (part + 1) * half)
            conv = mm_nt(unit, arrived[:, part].reshape(width, half).astype(BF16))
            product = k_ref[at, cut].astype(F32) * v_ref[at, cut].astype(F32)
            gated = q_ref[at, cut].astype(F32) * (conv + skip_ref[:, cut] * product)
            gall[n, at, lanes] = gated.astype(BF16)

        for part in range(PARTS):
            @pl.loop(1, y_count)
            def _(j):
                gated_copy(n, part, lanes, y_peer(j)).start()

    def wait_gated(n, part):
        all_gated(n, part).wait_recv()

    tile = min(cols, 512)
    tiles = cols // tile

    def term(n, at, lanes):
        return mm(gall[n, at], wall[n, :, :, lanes].reshape(y_count * width, tile))

    def tile_at(side, step):
        return pl.ds(pl.multiple_of(side * cols + step * tile, tile), tile)

    def rows_of(part, size):
        return slice(part * size, (part + 1) * size)

    def own_out(part):
        at = pl.ds(part * half, half)
        return pltpu.make_async_copy(acc.at[at], own_ref.at[at], own_sem.at[part])

    def project_first():
        for part in range(PARTS):
            wait_gated(0, part)

        @pl.loop(0, tiles)
        def _(step):
            acc[:, tile_at(0, step)] = term(0, slice(None), tile_at(1, step))

    def project_last():
        for part in range(PARTS):
            at = rows_of(part, part_rows)
            wait_gated(1, part)

            @pl.loop(0, tiles)
            def _(step):
                psend[at, tile_at(0, step)] = (acc[at, tile_at(0, step)] + term(1, at, tile_at(1, step))).astype(BF16)

            partial_copy(part).start()

        for part in range(2):
            at = rows_of(part, half)

            @pl.loop(0, tiles)
            def _(step):
                acc[at, tile_at(0, step)] = term(0, at, tile_at(0, step)) + term(1, at, tile_at(0, step))

            own_out(part).start()

        for part in range(2):
            own_out(part).wait()
        for part in range(PARTS):
            partial_copy(part).wait_recv()

    start_blocks(0)
    prepare(1)
    start_blocks(1)
    start_w(1)
    start_w(0)
    own_copy(0).start()
    own_copy(1).start()
    for load in loads[3:]:
        load.wait()
    convolve(0)
    share_w()
    convolve(1, lambda: gate(0))
    finish_w()
    gate(1)
    project_first()
    project_last()

    for n in range(CHUNKS):
        all_blocks(n).wait_send()
        all_back(n).wait_send()

    for n in range(CHUNKS):
        for part in range(PARTS):
            all_gated(n, part).wait_send()
    for kind in range(2):
        all_w(kind).wait_send()
        all_pass(kind).wait_send()
    for part in range(PARTS):
        partial_copy(part).wait_send()


def on_device(seq_count, chan_count, query_rows, key_rows, value_rows, filter_taps, skip_gain, w_out):
    rows, channels = query_rows.shape
    cols = w_out.shape[1] // chan_count
    width = channels // CHUNKS
    per = width // seq_count
    y_count = chan_count // 2
    tables = [jnp.asarray(t) for t in transform_tables(seq_count, rows // LANES)]
    anywhere = pl.BlockSpec(memory_space=pl.ANY)
    dma = pltpu.SemaphoreType.DMA
    operands = (query_rows, key_rows, value_rows, filter_taps, skip_gain.reshape(1, channels))
    own, other = pl.pallas_call(
        functools.partial(kernel, seq_count, chan_count),
        out_shape=(jax.ShapeDtypeStruct((rows, cols), F32), jax.ShapeDtypeStruct((rows, cols), BF16)),
        in_specs=[anywhere] * 10,
        out_specs=(anywhere, anywhere),
        scratch_shapes=[
            *(pltpu.VMEM(x.shape, x.dtype) for x in (*operands, *tables)),
            dma((9,)),
            pltpu.VMEM((CHUNKS, seq_count, 2 * per, rows), BF16),
            pltpu.VMEM((CHUNKS, seq_count, 2 * per, rows), BF16),
            pltpu.VMEM((rows // LANES, seq_count * 2 * per, LANES), F32),
            pltpu.VMEM((CHUNKS, seq_count, 2 * per, rows // 2), BF16),
            pltpu.VMEM((CHUNKS, seq_count, 2 * per, rows // 2), BF16),
            pltpu.VMEM((2, seq_count * 2 * per, LANES), F32),
            pltpu.VMEM((CHUNKS, rows, y_count * width), BF16),
            pltpu.VMEM((CHUNKS, y_count, width, 2 * cols), BF16),
            pltpu.VMEM((rows, cols), F32),
            pltpu.VMEM((rows, cols), BF16),
            dma((CHUNKS,)), dma((CHUNKS,)), dma((CHUNKS,)), dma((CHUNKS,)),
            dma((CHUNKS, PARTS)), dma((CHUNKS, PARTS)), dma((PARTS,)), dma((PARTS,)),
            dma((2,)), dma((2,)), dma((2,)), dma((2,)), dma((2,)), dma((2,)),
        ],
        compiler_params=pltpu.CompilerParams(
            collective_id=0, has_side_effects=True, vmem_limit_bytes=56 * 1024 * 1024),
    )(*operands, w_out.reshape(CHUNKS, width, w_out.shape[1]), *tables)
    return (own + other.astype(F32)).astype(BF16)


def solution(mesh):
    return jax.shard_map(
        functools.partial(on_device, mesh.shape["seq"], mesh.shape["chan"]),
        mesh=mesh,
        in_specs=(
            P("seq", "chan"),
            P("seq", "chan"),
            P("seq", "chan"),
            P("seq", "chan"),
            P("chan"),
            P("chan", None),
        ),
        out_specs=P("seq", "chan"),
        check_vma=False,
    )
```

time: 99.7 us -> 95.8 us (0.961)
  Pallas kernels: 97.3 us -> 92 us
  other arithmetic: 0 us -> 3.18 us
  local copies, waits for them, and re-layouts: 2.26 us -> 0 us
    pallas_call x1, Pallas kernels: 97.3 us -> 92 us  [on_device(): pl.pallas_call(functools.partial(kernel, seq_count, chan_count), out_shap...]
    convert_element_type x0 -> x1, other arithmetic: none -> 3.18 us  [on_device(): return (own + other.astype(F32)).astype(BF16)]
    unnamed x1 -> x0, local copies, waits for them, and re-layouts: 2.26 us -> none
where the time goes in v3:
time: 95.8 us; the launch traced here: 95.2 us
  Pallas kernels  92 us (96%)
  other arithmetic  3.18 us (3%)
    pallas_call x1, Pallas kernels, on_device(): pl.pallas_call(functools.partial(kernel, seq_count, chan_count), out_shap...  92 us
    convert_element_type x1, other arithmetic, on_device(): return (own + other.astype(F32)).astype(BF16)  3.18 us

profile of v3, /device:TPU:2, one launch (start us, length us, event | category | flops | bytes accessed | tf_op | source)
XLA Modules:
  0.0 95.2 jit_solution(16908653095700127085)
XLA Ops:
  0.0 92.0 %shard_map.100 = (f32[512,1024]{1,0:T(8,128)}, bf16[512,1024]{1,0:T(8,128)(2,1)}) custom-call(bf16[512,512]{1,0:T(8,128)(2,1)} %q_hbm.1, bf16[512,512]{1,0:T(8,128)(2,1)} %k_hbm.1, bf16[512,512]{1,0:T(8,128)(2,1)} %v_hbm.1, f32[512,512]{1,0:T(8,128)} %h_hbm.1, f32[1,512]{1,0:T(1,128)} %bitcast.3, bf16[2,256,8192]{2,1,0:T(8,128)(2,1)} %bitcast.2, ...), custom_call_target="tpu_custom_call" | custom-call | tf_op jit(solution)/shard_map/pallas_call | solution.py:427
  92.0 3.2 %add_convert_fusion = bf16[512,1024]{1,0:T(8,128)(2,1)} fusion(f32[512,1024]{1,0:T(8,128)} %get-tuple-element.7, bf16[512,1024]{1,0:T(8,128)(2,1)} %get-tuple-element.8), kind=kLoop, calls=%fused_computation | loop fusion | flops 1572864 | bytes 4194304 | tf_op jit(solution)/shard_map/convert_element_type | solution.py:452

commit v4 on v3

v4 whole, which is shorter than its diff:
```python
import functools

import jax
import jax.numpy as jnp
import ml_dtypes
import numpy as np
from jax import lax
from jax.experimental import pallas as pl
from jax.experimental.pallas import tpu as pltpu
from jax.sharding import PartitionSpec as P

MESH = pl.DeviceIdType.MESH
LANES = 128
CHUNKS = 4
PARTS = 4
BF16 = jnp.bfloat16
F32 = jnp.float32


def split_table(table):
    high = table.astype(ml_dtypes.bfloat16)
    low = (table - high.astype(np.float64)).astype(ml_dtypes.bfloat16)
    return high, low


def transform_tables(seq_count, row_groups):
    coarse = seq_count * row_groups
    total = coarse * LANES
    freq = np.arange(coarse) + 0.25
    order = (np.arange(seq_count)[None, :] * row_groups + np.arange(row_groups)[:, None]).reshape(-1)
    angle = 2.0 * np.pi * freq[:, None] * order[None, :] / coarse
    forward_first = np.concatenate((np.cos(angle), -np.sin(angle)), axis=0)
    inverse_first = np.concatenate((np.cos(angle).T, -np.sin(angle).T), axis=1) / total
    fine = np.arange(LANES)
    turn = 2.0 * np.pi * freq[:, None] * fine[None, :] / total
    twist_cos = np.cos(turn).astype(np.float32)
    twist_sin = np.sin(turn).astype(np.float32)
    inner = 2.0 * np.pi * (fine[:, None] * fine[None, :] % LANES) / LANES
    cosine, sine = np.cos(inner), np.sin(inner)
    forward_second = np.block([[cosine, -sine], [sine, cosine]])
    inverse_second = np.block([[cosine, sine], [-sine, cosine]])
    turns = np.stack((twist_cos, twist_sin))
    inner = np.stack((*split_table(forward_second), *split_table(inverse_second)))
    first = np.concatenate(split_table(forward_first), axis=1)
    last = np.stack(split_table(inverse_first))
    return turns, inner, first, last


def mm(left, right):
    return jnp.dot(left, right, preferred_element_type=F32)


def mm_nt(left, right):
    return lax.dot_general(left, right, (((1,), (1,)), ((), ())), preferred_element_type=F32)


def split(value):
    high = value.astype(BF16)
    low = (value - high.astype(F32)).astype(BF16)
    return high, low


def eye(size):
    row = lax.broadcasted_iota(jnp.int32, (size, size), 0)
    col = lax.broadcasted_iota(jnp.int32, (size, size), 1)
    return (row == col).astype(F32).astype(BF16)


def by_owner(seq_count, per):
    width = seq_count * per
    row = lax.broadcasted_iota(jnp.int32, (2 * width, 2 * width), 0)
    col = lax.broadcasted_iota(jnp.int32, (2 * width, 2 * width), 1)
    picked = row // per % 2 * width + row % per * seq_count + row // (2 * per)
    return (picked == col).astype(F32).astype(BF16)


def kernel(
    seq_count, chan_count,
    q_hbm, k_hbm, v_hbm, h_hbm, skip_hbm, w_ref, turns_hbm, inner_hbm, first_hbm, last_hbm,
    own_ref, precv,
    q_ref, k_ref, v_ref, h_ref, skip_ref, turns_ref, inner_ref, first_ref, last_ref, load_sem,
    send, recv, staged, zhi, zlo, yhi, ylo, ehi, elo, ysend, yrecv, ybuf, gall, wall, psend,
    send_sem, recv_sem, ysend_sem, yrecv_sem, gsend_sem, grecv_sem, psend_sem, precv_sem,
    wsend_sem, wrecv_sem, fsend_sem, frecv_sem, wown_sem,
):
    rows, channels = q_ref.shape
    groups = rows // LANES
    width = channels // CHUNKS
    per = width // seq_count
    coarse = seq_count * groups
    cols = own_ref.shape[1]
    y_count = chan_count // 2
    half = rows // 2
    levels = seq_count // 4
    part_rows = rows // PARTS
    me = lax.axis_index("seq")
    chan = lax.axis_index("chan")
    core = me % 2
    x_lo = (me // 2) % 2
    sibling = me + 1 - 2 * core
    mate = me + 2 - 4 * x_lo
    x_hi = chan // y_count
    y = chan % y_count
    facing = (1 - x_hi) * y_count + y

    def y_peer(j):
        return (y + j) % y_count

    def partner(j):
        group = (j + j // (seq_count - 4)) // 4
        shift = (group // 2 + 1) * (1 - 2 * (group % 2)) * (1 - group // (levels - 1))
        turn = (j + j // (seq_count - 4)) % 4
        return (me // 4 + shift + levels) % levels * 4 + (me % 4 + turn) % 4

    def device(seq_to, chan_to):
        return {"seq": seq_to, "chan": chan_to}

    barrier = pltpu.get_barrier_semaphore()

    @pl.loop(1, seq_count)
    def _(j):
        pl.semaphore_signal(barrier, inc=1, device_id=device((me + j) % seq_count, chan), device_id_type=MESH)

    @pl.loop(1, y_count)
    def _(j):
        pl.semaphore_signal(barrier, inc=1, device_id=device(me, x_hi * y_count + y_peer(j)), device_id_type=MESH)

    pl.semaphore_signal(barrier, inc=1, device_id=device(me, facing), device_id_type=MESH)

    loads = [pltpu.make_async_copy(source, target, load_sem.at[i]) for i, (source, target) in enumerate((
        (k_hbm, k_ref), (v_hbm, v_ref), (h_hbm, h_ref), (turns_hbm, turns_ref), (inner_hbm, inner_ref),
        (first_hbm, first_ref), (last_hbm, last_ref), (q_hbm, q_ref), (skip_hbm, skip_ref)))]
    for load in loads:
        load.start()
    for load in loads[:3]:
        load.wait()

    def prepare(n):
        cut = slice(n * width, (n + 1) * width)
        product = (k_ref[:, cut].astype(F32) * v_ref[:, cut].astype(F32)).astype(BF16)
        both = jnp.concatenate((product, h_ref[:, cut].astype(BF16)), axis=1)
        ordered = mm_nt(by_owner(seq_count, per), both).reshape(seq_count, 2 * per, rows)
        send[n] = jnp.concatenate((ordered[:, :, :half], ordered[:, :, half:]), axis=1).astype(BF16)

    prepare(0)
    pl.semaphore_wait(barrier, seq_count + y_count - 1)

    def block_copy(n, slot_out, slot_in, to):
        return pltpu.make_async_remote_copy(
            src_ref=send.at[n, slot_out], dst_ref=recv.at[n, slot_in],
            send_sem=send_sem.at[n], recv_sem=recv_sem.at[n],
            device_id={"seq": to, "chan": chan}, device_id_type=MESH)

    def back_copy(n, slot_out, slot_in, to):
        return pltpu.make_async_remote_copy(
            src_ref=ysend.at[n, slot_out], dst_ref=yrecv.at[n, slot_in],
            send_sem=ysend_sem.at[n], recv_sem=yrecv_sem.at[n],
            device_id={"seq": to, "chan": chan}, device_id_type=MESH)

    def gated_copy(n, part, lanes, to):
        block = gall.at[pl.ds(part * part_rows, part_rows), lanes]
        return pltpu.make_async_remote_copy(
            src_ref=block, dst_ref=block,
            send_sem=gsend_sem.at[n, part], recv_sem=grecv_sem.at[n, part],
            device_id=device(me, x_hi * y_count + to), device_id_type=MESH)

    def all_gated(n, part):
        return gated_copy(n, part, pl.ds(0, (y_count - 1) * width), y)

    def partial_copy(part):
        at = pl.ds(part * part_rows, part_rows)
        return pltpu.make_async_remote_copy(
            src_ref=psend.at[at], dst_ref=precv.at[at],
            send_sem=psend_sem.at[part], recv_sem=precv_sem.at[part],
            device_id=device(me, facing), device_id_type=MESH)

    core_rows = width // 2
    by_pair = width // 8
    first_half, last_half = pl.ds(0, CHUNKS // 2), pl.ds(CHUNKS // 2, CHUNKS // 2)
    w_chunks = (pl.ds(0, CHUNKS), pl.ds(0, CHUNKS), first_half, last_half)
    w_rows = (by_pair, core_rows - 2 * by_pair, core_rows // 2, core_rows)
    w_side = (1, 1, 0, 0)

    def w_start(kind):
        return core * core_rows + (x_lo * by_pair, 2 * by_pair, x_lo * (core_rows // 2), 0)[kind]

    def some_rows(start, size):
        return pl.ds(pl.multiple_of(start, 16), size)

    def lanes_of(side):
        return pl.ds(side * cols, cols)

    def side_of(col_side, x_side, y_side):
        target = jnp.where(col_side == 0, x_side, 1 - x_side)
        return pl.ds(pl.multiple_of((target * y_count + y_side) * cols, cols), cols)

    def w_copy(kind, to):
        at, side = some_rows(w_start(kind), w_rows[kind]), w_side[kind]
        return pltpu.make_async_remote_copy(
            src_ref=w_ref.at[w_chunks[kind], at, side_of(side, x_hi, to)], dst_ref=wall.at[w_chunks[kind], y, at, lanes_of(side)],
            send_sem=wsend_sem.at[kind], recv_sem=wrecv_sem.at[kind],
            device_id=device(me, x_hi * y_count + to), device_id_type=MESH)

    def all_w(kind):
        block = wall.at[w_chunks[kind], pl.ds(0, y_count - 1), pl.ds(0, w_rows[kind]), lanes_of(0)]
        return pltpu.make_async_remote_copy(
            src_ref=block, dst_ref=block, send_sem=wsend_sem.at[kind], recv_sem=wrecv_sem.at[kind],
            device_id=device(me, facing), device_id_type=MESH)

    pass_rows = (by_pair, core_rows // 2, core_rows, core_rows, core_rows)
    pass_side = (1, 0, 1, 0, 0)
    pass_chunks = (pl.ds(0, CHUNKS), first_half, pl.ds(0, CHUNKS), first_half, last_half)
    pass_to = (mate, mate, sibling, sibling, sibling)

    def w_pass(route, slot):
        start = core * core_rows + (x_lo * pass_rows[route] if route < 2 else 0)
        block = wall.at[pass_chunks[route], slot, some_rows(start, pass_rows[route]), lanes_of(pass_side[route])]
        return pltpu.make_async_remote_copy(
            src_ref=block, dst_ref=block, send_sem=fsend_sem.at[route], recv_sem=frecv_sem.at[route],
            device_id=device(pass_to[route], chan), device_id_type=MESH)

    def all_pass(route):
        block = wall.at[pass_chunks[route], pl.ds(0, y_count - 1), pl.ds(0, pass_rows[route]), lanes_of(0)]
        return pltpu.make_async_remote_copy(
            src_ref=block, dst_ref=block, send_sem=fsend_sem.at[route], recv_sem=frecv_sem.at[route],
            device_id=device(pass_to[route], chan), device_id_type=MESH)

    def own_copy(col_side):
        return pltpu.make_async_copy(
            w_ref.at[:, :, side_of(col_side, x_hi, y)],
            wall.at[:, y, :, pl.ds(col_side * cols, cols)], wown_sem.at[col_side])

    def start_w(kind):
        @pl.loop(1, y_count)
        def _(j):
            w_copy(kind, y_peer(j)).start()

    def start_pass(route):
        @pl.loop(1, y_count)
        def _(j):
            w_pass(route, y_peer(j)).start()

    def start_blocks(n):
        @pl.loop(0, seq_count - 1)
        def _(j):
            to = partner(j)
            block_copy(n, to, me, to).start()
        recv[n, me] = send[n, me]

    others = pl.ds(0, seq_count - 1)

    def all_blocks(n):
        return block_copy(n, others, others, me)

    def all_back(n):
        return back_copy(n, others, others, me)

    def convolve(n):
        all_blocks(n).wait_recv()
        if n + 2 < CHUNKS:
            start_blocks(n + 2)

        for g in range(2):
            staged[g] = recv[n, :, :, g * LANES:(g + 1) * LANES].astype(F32).reshape(seq_count * 4 * per, LANES)

        def gather_rows(row):
            parts = [staged[g % 2, pl.ds(g // 2 * 2 * per + row, seq_count, stride=4 * per)] for g in range(groups)]
            return jnp.concatenate(parts, axis=0)

        cosine, sine = turns_ref[0], turns_ref[1]
        cosines, sines = jnp.concatenate((cosine, cosine), axis=1), jnp.concatenate((sine, sine), axis=1)
        for c in range(per):
            signal = jnp.concatenate((gather_rows(c), gather_rows(c + per)), axis=1).astype(BF16)
            stage = mm(first_ref[...], jnp.concatenate((signal, signal), axis=0))
            real, imag = stage[:coarse], stage[coarse:]
            turned_re = real * cosines + imag * sines
            turned_im = imag * cosines - real * sines
            for side in range(2):
                at = slice((2 * c + side) * coarse, (2 * c + side + 1) * coarse)
                lanes = slice(side * LANES, (side + 1) * LANES)
                zhi[at, :LANES], zlo[at, :LANES] = split(turned_re[:, lanes])
                zhi[at, LANES:], zlo[at, LANES:] = split(turned_im[:, lanes])

        group = min(per, 4)
        for t in range(per // group):
            at = slice(2 * group * t * coarse, 2 * group * (t + 1) * coarse)
            high, low = zhi[at], zlo[at]
            both = mm(high, inner_ref[0]) + mm(low, inner_ref[0]) + mm(high, inner_ref[1])
            for c in range(group):
                p_re, p_im = both[2 * c * coarse:(2 * c + 1) * coarse, :LANES], both[2 * c * coarse:(2 * c + 1) * coarse, LANES:]
                h_re, h_im = both[(2 * c + 1) * coarse:(2 * c + 2) * coarse, :LANES], both[(2 * c + 1) * coarse:(2 * c + 2) * coarse, LANES:]
                at = slice((t * group + c) * coarse, (t * group + c + 1) * coarse)
                yhi[at, :LANES], ylo[at, :LANES] = split(p_re * h_re - p_im * h_im)
                yhi[at, LANES:], ylo[at, LANES:] = split(p_re * h_im + p_im * h_re)

        for t in range(per // group):
            at = slice(group * t * coarse, group * (t + 1) * coarse)
            high, low = yhi[at], ylo[at]
            back = mm(high, inner_ref[2]) + mm(low, inner_ref[2]) + mm(high, inner_ref[3])
            for c in range(group):
                real, imag = back[c * coarse:(c + 1) * coarse, :LANES], back[c * coarse:(c + 1) * coarse, LANES:]
                lanes = slice((t * group + c) * LANES, (t * group + c + 1) * LANES)
                ehi[:coarse, lanes], elo[:coarse, lanes] = split(real * cosine - imag * sine)
                ehi[coarse:, lanes], elo[coarse:, lanes] = split(imag * cosine + real * sine)

        for t in range(per // group):
            lanes = slice(group * t * LANES, group * (t + 1) * LANES)
            high, low = ehi[:, lanes], elo[:, lanes]
            result = mm(last_ref[0], high) + mm(last_ref[0], low) + mm(last_ref[1], high)
            for c in range(group):
                for g in range(groups):
                    ybuf[pl.ds(g * per + t * group + c, seq_count, stride=4 * per)] = (
                        result[g * seq_count:(g + 1) * seq_count, c * LANES:(c + 1) * LANES])

        ysend[n] = ybuf[...].astype(BF16).reshape(seq_count, 4 * per, LANES)

        @pl.loop(0, seq_count - 1)
        def _(j):
            to = partner(j)
            back_copy(n, to, me, to).start()
        yrecv[n, me] = ysend[n, me]

    def gate(n):
        all_back(n).wait_recv()

        cut = slice(n * width, (n + 1) * width)
        ybuf[...] = yrecv[n].astype(F32).reshape(seq_count * 4 * per, LANES)
        arrived = [ybuf[pl.ds(row, seq_count, stride=4 * per)] for row in range(4 * per)]
        turned = mm_nt(eye(LANES), jnp.concatenate(arrived, axis=0).astype(BF16))
        lanes = pl.ds(pl.multiple_of(n * y_count * width + y * width, width), width)
        for g in range(groups):
            at = slice(g * LANES, (g + 1) * LANES)
            product = k_ref[at, cut].astype(F32) * v_ref[at, cut].astype(F32)
            conv = turned[:, g * width:(g + 1) * width]
            gated = q_ref[at, cut].astype(F32) * (conv + skip_ref[:, cut] * product)
            gall[at, lanes] = gated.astype(BF16)

    def send_gated(n, part):
        lanes = pl.ds(pl.multiple_of(n * y_count * width + y * width, width), width)

        @pl.loop(1, y_count)
        def _(j):
            gated_copy(n, part, lanes, y_peer(j)).start()

    def wait_gated(n, part):
        all_gated(n, part).wait_recv()

    tile = min(cols, 512)
    tiles = cols // tile

    depth = y_count * width

    def term(first, last, at, lanes):
        left = gall[at, first * depth:last * depth]
        return mm(left, wall[first:last, :, :, lanes].reshape((last - first) * depth, tile))

    def tile_at(side, step):
        return pl.ds(pl.multiple_of(side * cols + step * tile, tile), tile)

    def rows_of(part, size):
        return slice(part * size, (part + 1) * size)

    def project_other(part):
        at = rows_of(part, part_rows)
        for n in range(CHUNKS):
            wait_gated(n, part)

        @pl.loop(0, tiles)
        def _(step):
            psend[at, tile_at(0, step)] = term(0, CHUNKS, at, tile_at(1, step)).astype(BF16)

        partial_copy(part).start()

    def project_own():
        own_copy(0).wait()
        all_pass(3).wait_recv()
        for part in range(2):
            at = rows_of(part, half)

            @pl.loop(0, tiles)
            def _(step):
                own_ref[at, tile_at(0, step)] = term(0, CHUNKS // 2, at, tile_at(0, step))

        all_w(3).wait_recv()
        start_pass(4)
        all_pass(4).wait_recv()
        for part in range(2):
            at = rows_of(part, half)

            @pl.loop(0, tiles)
            def _(step):
                own_ref[at, tile_at(0, step)] += term(CHUNKS // 2, CHUNKS, at, tile_at(0, step))

    start_blocks(0)
    prepare(1)
    start_blocks(1)
    start_w(0)
    start_w(1)
    start_w(2)
    own_copy(1).start()
    own_copy(0).start()
    for n in range(2, CHUNKS):
        prepare(n)
    for load in loads[3:]:
        load.wait()
    convolve(0)
    all_w(0).wait_recv()
    start_pass(0)
    convolve(1)
    convolve(2)
    gate(0)
    for part in range(PARTS):
        send_gated(0, part)
    convolve(3)
    all_w(2).wait_recv()
    start_pass(1)
    all_w(1).wait_recv()
    all_pass(0).wait_recv()
    start_pass(2)
    gate(1)
    for part in range(3):
        send_gated(1, part)
    gate(2)
    for part in range(2):
        send_gated(2, part)
    gate(3)
    for n, part in ((3, 0), (3, 1), (2, 2), (3, 2), (1, 3), (2, 3), (3, 3)):
        send_gated(n, part)
    start_w(3)
    all_pass(1).wait_recv()
    start_pass(3)
    own_copy(1).wait()
    all_pass(2).wait_recv()
    for part in range(PARTS):
        project_other(part)
    project_own()
    for part in range(PARTS):
        partial_copy(part).wait_recv()

    for n in range(CHUNKS):
        all_blocks(n).wait_send()
        all_back(n).wait_send()

    for n in range(CHUNKS):
        for part in range(PARTS):
            all_gated(n, part).wait_send()
    for kind in range(4):
        all_w(kind).wait_send()
    for route in range(5):
        all_pass(route).wait_send()
    for part in range(PARTS):
        partial_copy(part).wait_send()


def on_device(seq_count, chan_count, query_rows, key_rows, value_rows, filter_taps, skip_gain, w_out):
    rows, channels = query_rows.shape
    cols = w_out.shape[1] // chan_count
    width = channels // CHUNKS
    per = width // seq_count
    y_count = chan_count // 2
    coarse = seq_count * rows // LANES
    tables = [jnp.asarray(t) for t in transform_tables(seq_count, rows // LANES)]
    anywhere = pl.BlockSpec(memory_space=pl.ANY)
    dma = pltpu.SemaphoreType.DMA
    operands = (query_rows, key_rows, value_rows, filter_taps, skip_gain.reshape(1, channels))
    own, other = pl.pallas_call(
        functools.partial(kernel, seq_count, chan_count),
        out_shape=(pltpu.VMEM((rows, cols), F32), pltpu.VMEM((rows, cols), BF16)),
        in_specs=[anywhere] * 10,
        out_specs=(pl.BlockSpec(memory_space=pltpu.VMEM),) * 2,
        scratch_shapes=[
            *(pltpu.VMEM(x.shape, x.dtype) for x in (*operands, *tables)),
            dma((9,)),
            pltpu.VMEM((CHUNKS, seq_count, 4 * per, rows // 2), BF16),
            pltpu.VMEM((CHUNKS, seq_count, 4 * per, rows // 2), BF16),
            pltpu.VMEM((2, seq_count * 4 * per, LANES), F32),
            *(pltpu.VMEM((2 * per * coarse, 2 * LANES), BF16) for _ in range(2)),
            *(pltpu.VMEM((per * coarse, 2 * LANES), BF16) for _ in range(2)),
            *(pltpu.VMEM((2 * coarse, per * LANES), BF16) for _ in range(2)),
            pltpu.VMEM((CHUNKS, seq_count, 4 * per, LANES), BF16),
            pltpu.VMEM((CHUNKS, seq_count, 4 * per, LANES), BF16),
            pltpu.VMEM((seq_count * 4 * per, LANES), F32),
            pltpu.VMEM((rows, CHUNKS * y_count * width), BF16),
            pltpu.VMEM((CHUNKS, y_count, width, 2 * cols), BF16),
            pltpu.VMEM((rows, cols), BF16),
            dma((CHUNKS,)), dma((CHUNKS,)), dma((CHUNKS,)), dma((CHUNKS,)),
            dma((CHUNKS, PARTS)), dma((CHUNKS, PARTS)), dma((PARTS,)), dma((PARTS,)),
            dma((4,)), dma((4,)), dma((5,)), dma((5,)), dma((2,)),
        ],
        compiler_params=pltpu.CompilerParams(
            collective_id=0, has_side_effects=True, vmem_limit_bytes=56 * 1024 * 1024),
    )(*operands, w_out.reshape(CHUNKS, width, w_out.shape[1]), *tables)
    return (own + other.astype(F32)).astype(BF16)


def solution(mesh):
    return jax.shard_map(
        functools.partial(on_device, mesh.shape["seq"], mesh.shape["chan"]),
        mesh=mesh,
        in_specs=(
            P("seq", "chan"),
            P("seq", "chan"),
            P("seq", "chan"),
            P("seq", "chan"),
            P("chan"),
            P("chan", None),
        ),
        out_specs=P("seq", "chan"),
        check_vma=False,
    )
```

time: 95.8 us -> 85.1 us (0.89)
  Pallas kernels: 92 us -> 82.2 us
  other arithmetic: 3.18 us -> 1.32 us
    pallas_call x1, Pallas kernels: 92 us -> 82.2 us  [on_device(): pl.pallas_call(functools.partial(kernel, seq_count, chan_count), out_shap...]
    convert_element_type x1, other arithmetic: 3.18 us -> 1.32 us  [on_device(): return (own + other.astype(F32)).astype(BF16)]
where the time goes in v4:
time: 85.1 us; the launch traced here: 83.5 us
  Pallas kernels  82.2 us (97%)
  other arithmetic  1.32 us (2%)
    pallas_call x1, Pallas kernels, on_device(): pl.pallas_call(functools.partial(kernel, seq_count, chan_count), out_shap...  82.2 us

profile of v4, /device:TPU:2, one launch (start us, length us, event | category | flops | bytes accessed | tf_op | source)
XLA Modules:
  0.0 83.5 jit_solution(14365464427653391922)
XLA Ops:
  0.0 82.2 %shard_map.100 = (f32[512,1024]{1,0:T(8,128)S(1)}, bf16[512,1024]{1,0:T(8,128)(2,1)S(1)}) custom-call(bf16[512,512]{1,0:T(8,128)(2,1)} %q_hbm.1, bf16[512,512]{1,0:T(8,128)(2,1)} %k_hbm.1, bf16[512,512]{1,0:T(8,128)(2,1)} %v_hbm.1, f32[512,512]{1,0:T(8,128)} %h_hbm.1, f32[1,512]{1,0:T(1,128)} %bitcast.3, bf16[4,128,8192]{2,1,0:T(8,128)(2,1)} %bitcast.2, ...), custom_call_target="tpu_custom_call" | custom-call | tf_op jit(solution)/shard_map/pallas_call | solution.py:466
  82.2 1.3 %add_convert_fusion = bf16[512,1024]{1,0:T(8,128)(2,1)} fusion(f32[512,1024]{1,0:T(8,128)S(1)} %get-tuple-element.7, bf16[512,1024]{1,0:T(8,128)(2,1)S(1)} %get-tuple-element.8), kind=kLoop, calls=%fused_computation | loop fusion | flops 1572864 | bytes 4194304 | tf_op jit(solution)/shard_map/convert_element_type | solution.py:493

commit v5 on v4

--- a/solution.py
+++ b/solution.py
@@ -79,7 +79,7 @@
     q_hbm, k_hbm, v_hbm, h_hbm, skip_hbm, w_ref, turns_hbm, inner_hbm, first_hbm, last_hbm,
     own_ref, precv,
     q_ref, k_ref, v_ref, h_ref, skip_ref, turns_ref, inner_ref, first_ref, last_ref, load_sem,
-    send, recv, staged, zhi, zlo, yhi, ylo, ehi, elo, ysend, yrecv, ybuf, gall, wall, psend,
+    send, recv, staged, zhi, zlo, yhi, ylo, ehi, elo, ysend, yrecv, ybuf, gall, wall, acc, psend,
     send_sem, recv_sem, ysend_sem, yrecv_sem, gsend_sem, grecv_sem, psend_sem, precv_sem,
     wsend_sem, wrecv_sem, fsend_sem, frecv_sem, wown_sem,
 ):
@@ -97,6 +97,9 @@
     chan = lax.axis_index("chan")
     core = me % 2
     x_lo = (me // 2) % 2
+    parity = (me // 4) % 2
+    above = (me + 4) % seq_count
+    below = (me + seq_count - 4) % seq_count
     sibling = me + 1 - 2 * core
     mate = me + 2 - 4 * x_lo
     x_hi = chan // y_count
@@ -178,11 +181,11 @@
     by_pair = width // 8
     first_half, last_half = pl.ds(0, CHUNKS // 2), pl.ds(CHUNKS // 2, CHUNKS // 2)
     w_chunks = (pl.ds(0, CHUNKS), pl.ds(0, CHUNKS), first_half, last_half)
-    w_rows = (by_pair, core_rows - 2 * by_pair, core_rows // 2, core_rows)
+    w_rows = (by_pair, core_rows - 2 * by_pair, core_rows // 2, core_rows // 2)
     w_side = (1, 1, 0, 0)
 
     def w_start(kind):
-        return core * core_rows + (x_lo * by_pair, 2 * by_pair, x_lo * (core_rows // 2), 0)[kind]
+        return core * core_rows + (x_lo * by_pair, 2 * by_pair, parity * (core_rows // 2), parity * (core_rows // 2))[kind]
 
     def some_rows(start, size):
         return pl.ds(pl.multiple_of(start, 16), size)
@@ -207,13 +210,16 @@
             src_ref=block, dst_ref=block, send_sem=wsend_sem.at[kind], recv_sem=wrecv_sem.at[kind],
             device_id=device(me, facing), device_id_type=MESH)
 
-    pass_rows = (by_pair, core_rows // 2, core_rows, core_rows, core_rows)
-    pass_side = (1, 0, 1, 0, 0)
-    pass_chunks = (pl.ds(0, CHUNKS), first_half, pl.ds(0, CHUNKS), first_half, last_half)
-    pass_to = (mate, mate, sibling, sibling, sibling)
+    quarter = core_rows // 4
+    pass_rows = (by_pair, quarter, quarter, quarter, core_rows, core_rows, core_rows, quarter)
+    pass_side = (1, 0, 0, 0, 1, 0, 0, 0)
+    every = pl.ds(0, CHUNKS)
+    pass_chunks = (every, first_half, last_half, last_half, every, first_half, last_half, first_half)
+    pass_to = (mate, above, above, below, sibling, sibling, sibling, below)
 
     def w_pass(route, slot):
-        start = core * core_rows + (x_lo * pass_rows[route] if route < 2 else 0)
+        up, down = parity * 2 * quarter, (parity * 2 + 1) * quarter
+        start = core * core_rows + (x_lo * by_pair, up, up, down, 0, 0, 0, down)[route]
         block = wall.at[pass_chunks[route], slot, some_rows(start, pass_rows[route]), lanes_of(pass_side[route])]
         return pltpu.make_async_remote_copy(
             src_ref=block, dst_ref=block, send_sem=fsend_sem.at[route], recv_sem=frecv_sem.at[route],
@@ -360,36 +366,40 @@
     def rows_of(part, size):
         return slice(part * size, (part + 1) * size)
 
+    def project_ahead():
+        for n in range(2):
+            for part in range(2):
+                wait_gated(n, part)
+
+        @pl.loop(0, tiles)
+        def _(step):
+            acc[:, tile_at(0, step)] = term(0, 2, slice(0, half), tile_at(1, step))
+
     def project_other(part):
         at = rows_of(part, part_rows)
-        for n in range(CHUNKS):
+        for n in range(2 if part < 2 else 0, CHUNKS):
             wait_gated(n, part)
 
         @pl.loop(0, tiles)
         def _(step):
-            psend[at, tile_at(0, step)] = term(0, CHUNKS, at, tile_at(1, step)).astype(BF16)
+            if part < 2:
+                total = acc[at, tile_at(0, step)] + term(2, CHUNKS, at, tile_at(1, step))
+            else:
+                total = term(0, CHUNKS, at, tile_at(1, step))
+            psend[at, tile_at(0, step)] = total.astype(BF16)
 
         partial_copy(part).start()
 
     def project_own():
         own_copy(0).wait()
-        all_pass(3).wait_recv()
+        all_pass(5).wait_recv()
+        all_pass(6).wait_recv()
         for part in range(2):
             at = rows_of(part, half)
 
             @pl.loop(0, tiles)
             def _(step):
-                own_ref[at, tile_at(0, step)] = term(0, CHUNKS // 2, at, tile_at(0, step))
-
-        all_w(3).wait_recv()
-        start_pass(4)
-        all_pass(4).wait_recv()
-        for part in range(2):
-            at = rows_of(part, half)
-
-            @pl.loop(0, tiles)
-            def _(step):
-                own_ref[at, tile_at(0, step)] += term(CHUNKS // 2, CHUNKS, at, tile_at(0, step))
+                own_ref[at, tile_at(0, step)] = term(0, CHUNKS, at, tile_at(0, step))
 
     start_blocks(0)
     prepare(1)
@@ -404,35 +414,49 @@
     for load in loads[3:]:
         load.wait()
     convolve(0)
+    convolve(1)
     all_w(0).wait_recv()
     start_pass(0)
-    convolve(1)
     convolve(2)
     gate(0)
     for part in range(PARTS):
         send_gated(0, part)
     convolve(3)
-    all_w(2).wait_recv()
-    start_pass(1)
     all_w(1).wait_recv()
     all_pass(0).wait_recv()
-    start_pass(2)
+    start_pass(4)
     gate(1)
-    for part in range(3):
+    for part in range(2):
         send_gated(1, part)
     gate(2)
     for part in range(2):
         send_gated(2, part)
+    own_copy(1).wait()
+    all_pass(4).wait_recv()
+    project_ahead()
     gate(3)
-    for n, part in ((3, 0), (3, 1), (2, 2), (3, 2), (1, 3), (2, 3), (3, 3)):
-        send_gated(n, part)
+    send_gated(3, 0)
+    send_gated(3, 1)
     start_w(3)
+    all_w(2).wait_recv()
+    start_pass(1)
+    start_pass(7)
+    for part in range(2, PARTS):
+        for n in range(1, CHUNKS):
+            send_gated(n, part)
+    project_other(0)
+    project_other(1)
     all_pass(1).wait_recv()
+    all_pass(7).wait_recv()
+    start_pass(5)
+    all_w(3).wait_recv()
+    start_pass(2)
     start_pass(3)
-    own_copy(1).wait()
+    project_other(2)
     all_pass(2).wait_recv()
-    for part in range(PARTS):
-        project_other(part)
+    all_pass(3).wait_recv()
+    start_pass(6)
+    project_other(3)
     project_own()
     for part in range(PARTS):
         partial_copy(part).wait_recv()
@@ -446,7 +470,7 @@
             all_gated(n, part).wait_send()
     for kind in range(4):
         all_w(kind).wait_send()
-    for route in range(5):
+    for route in range(8):
         all_pass(route).wait_send()
     for part in range(PARTS):
         partial_copy(part).wait_send()
@@ -482,10 +506,11 @@
             pltpu.VMEM((seq_count * 4 * per, LANES), F32),
             pltpu.VMEM((rows, CHUNKS * y_count * width), BF16),
             pltpu.VMEM((CHUNKS, y_count, width, 2 * cols), BF16),
+            pltpu.VMEM((rows // 2, cols), F32),
             pltpu.VMEM((rows, cols), BF16),
             dma((CHUNKS,)), dma((CHUNKS,)), dma((CHUNKS,)), dma((CHUNKS,)),
             dma((CHUNKS, PARTS)), dma((CHUNKS, PARTS)), dma((PARTS,)), dma((PARTS,)),
-            dma((4,)), dma((4,)), dma((5,)), dma((5,)), dma((2,)),
+            dma((4,)), dma((4,)), dma((8,)), dma((8,)), dma((2,)),
         ],
         compiler_params=pltpu.CompilerParams(
             collective_id=0, has_side_effects=True, vmem_limit_bytes=56 * 1024 * 1024),

time: 85.1 us -> 82.1 us (0.965)
  Pallas kernels: 82.2 us -> 79.4 us
    pallas_call x1, Pallas kernels: 82.2 us -> 79.4 us  [on_device(): pl.pallas_call(functools.partial(kernel, seq_count, chan_count), out_shap...]
where the time goes in v5:
time: 82.1 us; the launch traced here: 80.7 us
  Pallas kernels  79.4 us (97%)
  other arithmetic  1.32 us (2%)
    pallas_call x1, Pallas kernels, on_device(): pl.pallas_call(functools.partial(kernel, seq_count, chan_count), out_shap...  79.4 us

profile of v5, /device:TPU:2, one launch (start us, length us, event | category | flops | bytes accessed | tf_op | source)
XLA Modules:
  0.0 80.7 jit_solution(232077540535738029)
XLA Ops:
  0.0 79.4 %shard_map.100 = (f32[512,1024]{1,0:T(8,128)S(1)}, bf16[512,1024]{1,0:T(8,128)(2,1)S(1)}) custom-call(bf16[512,512]{1,0:T(8,128)(2,1)} %q_hbm.1, bf16[512,512]{1,0:T(8,128)(2,1)} %k_hbm.1, bf16[512,512]{1,0:T(8,128)(2,1)} %v_hbm.1, f32[512,512]{1,0:T(8,128)} %h_hbm.1, f32[1,512]{1,0:T(1,128)} %bitcast.3, bf16[4,128,8192]{2,1,0:T(8,128)(2,1)} %bitcast.2, ...), custom_call_target="tpu_custom_call" | custom-call | tf_op jit(solution)/shard_map/pallas_call | solution.py:490
  79.4 1.3 %add_convert_fusion = bf16[512,1024]{1,0:T(8,128)(2,1)} fusion(f32[512,1024]{1,0:T(8,128)S(1)} %get-tuple-element.7, bf16[512,1024]{1,0:T(8,128)(2,1)S(1)} %get-tuple-element.8), kind=kLoop, calls=%fused_computation | loop fusion | flops 1572864 | bytes 4194304 | tf_op jit(solution)/shard_map/convert_element_type | solution.py:518

commit v6 on v5

--- a/solution.py
+++ b/solution.py
@@ -422,12 +422,12 @@
     for part in range(PARTS):
         send_gated(0, part)
     convolve(3)
+    gate(1)
+    for part in range(2):
+        send_gated(1, part)
     all_w(1).wait_recv()
     all_pass(0).wait_recv()
     start_pass(4)
-    gate(1)
-    for part in range(2):
-        send_gated(1, part)
     gate(2)
     for part in range(2):
         send_gated(2, part)

time: 82.1 us -> 82.3 us (level)
  no operation moved by 1% of the time
where the time goes in v6:
time: 82.3 us; the launch traced here: 81 us
  Pallas kernels  79.7 us (97%)
  other arithmetic  1.32 us (2%)
    pallas_call x1, Pallas kernels, on_device(): pl.pallas_call(functools.partial(kernel, seq_count, chan_count), out_shap...  79.7 us

profile of v6, /device:TPU:2, one launch (start us, length us, event | category | flops | bytes accessed | tf_op | source)
XLA Modules:
  0.0 81.0 jit_solution(2413954465457924341)
XLA Ops:
  0.0 79.7 %shard_map.100 = (f32[512,1024]{1,0:T(8,128)S(1)}, bf16[512,1024]{1,0:T(8,128)(2,1)S(1)}) custom-call(bf16[512,512]{1,0:T(8,128)(2,1)} %q_hbm.1, bf16[512,512]{1,0:T(8,128)(2,1)} %k_hbm.1, bf16[512,512]{1,0:T(8,128)(2,1)} %v_hbm.1, f32[512,512]{1,0:T(8,128)} %h_hbm.1, f32[1,512]{1,0:T(1,128)} %bitcast.3, bf16[4,128,8192]{2,1,0:T(8,128)(2,1)} %bitcast.2, ...), custom_call_target="tpu_custom_call" | custom-call | tf_op jit(solution)/shard_map/pallas_call | solution.py:490
  79.7 1.3 %add_convert_fusion = bf16[512,1024]{1,0:T(8,128)(2,1)} fusion(f32[512,1024]{1,0:T(8,128)S(1)} %get-tuple-element.7, bf16[512,1024]{1,0:T(8,128)(2,1)S(1)} %get-tuple-element.8), kind=kLoop, calls=%fused_computation | loop fusion | flops 1572864 | bytes 4194304 | tf_op jit(solution)/shard_map/convert_element_type | solution.py:518
